TPU v7x, 32 devices: a whole 2x2x4 slice. The times are simulated.
32 devices in a mesh: fsdp: 8 (over y, x, core), dp: 4 (over z).
Axes of the slice: x: 2, y: 2, z: 4, core: 2. Of those that a mesh axis runs over, the one named last changes fastest.
Arguments:
- inputs: bfloat16 [16, 2048, 768], P('dp', 'fsdp'), may hold values from -6 to 6
- cotangent: bfloat16 [16, 2048, 768], P('dp', 'fsdp'), may hold values from -6 to 6
- segments: int32 [16, 2048], P('dp'), may hold values from 0 to 2047, as said below
- norm1_gain: bfloat16 [768], P('fsdp'), may hold values from 0.5 to 1.5
- norm1_bias: bfloat16 [768], P('fsdp'), may hold values from -1 to 1
- qkv_weight: bfloat16 [768, 2304], P('fsdp'), may hold values from -0.21875 to 0.21875
- query_bias: bfloat16 [768], P('fsdp'), may hold values from -1 to 1
- value_bias: bfloat16 [768], P('fsdp'), may hold values from -1 to 1
- proj_weight: bfloat16 [768, 768], P('fsdp'), may hold values from -1.25 to 1.25
- proj_bias: bfloat16 [768], P('fsdp'), may hold values from -1 to 1
- norm2_gain: bfloat16 [768], P('fsdp'), may hold values from 0.5 to 1.5
- norm2_bias: bfloat16 [768], P('fsdp'), may hold values from -1 to 1
- up_weight: bfloat16 [768, 3072], P('fsdp'), may hold values from -0.21875 to 0.21875
- up_bias: bfloat16 [3072], P('fsdp'), may hold values from -1 to 1
- down_weight: bfloat16 [3072, 768], P('fsdp'), may hold values from -0.109375 to 0.109375
- down_bias: bfloat16 [768], P('fsdp'), may hold values from -1 to 1
Outputs:
- layer_out: bfloat16 [16, 2048, 768], P('dp', 'fsdp')
- input_grad: float32 [16, 2048, 768], P('dp', 'fsdp')
- norm1_gain_grad: float32 [768], P('fsdp')
- norm1_bias_grad: float32 [768], P('fsdp')
- qkv_weight_grad: float32 [768, 2304], P('fsdp')
- query_bias_grad: float32 [768], P('fsdp')
- value_bias_grad: float32 [768], P('fsdp')
- proj_weight_grad: float32 [768, 768], P('fsdp')
- proj_bias_grad: float32 [768], P('fsdp')
- norm2_gain_grad: float32 [768], P('fsdp')
- norm2_bias_grad: float32 [768], P('fsdp')
- up_weight_grad: float32 [768, 3072], P('fsdp')
- up_bias_grad: float32 [3072], P('fsdp')
- down_weight_grad: float32 [3072, 768], P('fsdp')
- down_bias_grad: float32 [768], P('fsdp')
Inputs may be any that keep to these rules, and one draw needn't show every extreme that they name: `segments`: along each sequence the document numbers never fall; tokens with equal numbers form one document, and each token's number is the position of its document's first token in the sequence; the last token of every sequence forms a document of its own. Among the 4 sequences of each index of dp one holds a document that begins within the first 256 tokens and ends within the last 256.
All inputs are finite; a program needn't handle non-finite values.
Results may differ from a plain program's by a relative error of at most 0.011.
Values may be sent and summed in bfloat16 or wider, within the bound.
A program may use at most 256 MiB of HBM per device.

v0:
```python
import jax
import jax.numpy as jnp
from jax import lax
from jax.sharding import PartitionSpec as P

HD = 64


def layer_norm_core(values, gains, shifts):
    centre = jnp.mean(values, axis=-1, keepdims=True)
    centred = values - centre
    spread = jnp.mean(centred * centred, axis=-1, keepdims=True)
    return centred * lax.rsqrt(spread + 1e-05) * gains + shifts


def smooth_gate(values):
    return jax.nn.gelu(values, approximate=True)


def pair_columns(source, pair_index, offset):
    first_col = offset + pair_index * 2 * HD
    picked = lax.dynamic_slice_in_dim(source, first_col, 2 * HD, 2)
    return picked.reshape(source.shape[0], source.shape[1], 2, HD)


def regroup(stacked):
    merged = jnp.transpose(stacked, (1, 2, 0, 3))
    return merged.reshape(stacked.shape[1], stacked.shape[2], stacked.shape[0] * stacked.shape[3])


def local(
    inputs,
    cotangent,
    segments,
    norm1_gain,
    norm1_bias,
    qkv_weight,
    query_bias,
    value_bias,
    proj_weight,
    proj_bias,
    norm2_gain,
    norm2_bias,
    up_weight,
    up_bias,
    down_weight,
    down_bias,
):
    seq_count, own_rows, model_width = inputs.shape
    length = segments.shape[1]
    pair_count = model_width // (2 * HD)
    token_count = seq_count * own_rows
    score_scale = HD ** (-0.5)
    first_row = lax.axis_index("fsdp") * own_rows
    (
        gain_one,
        shift_one,
        qkv_full,
        query_shift,
        value_shift,
        proj_full,
        proj_shift,
        gain_two,
        shift_two,
        up_full,
        up_shift,
        down_full,
        down_shift,
    ) = (
        lax.all_gather(norm1_gain, "fsdp", axis=0, tiled=True),
        lax.all_gather(norm1_bias, "fsdp", axis=0, tiled=True),
        lax.all_gather(qkv_weight, "fsdp", axis=0, tiled=True),
        lax.all_gather(query_bias, "fsdp", axis=0, tiled=True),
        lax.all_gather(value_bias, "fsdp", axis=0, tiled=True),
        lax.all_gather(proj_weight, "fsdp", axis=0, tiled=True),
        lax.all_gather(proj_bias, "fsdp", axis=0, tiled=True),
        lax.all_gather(norm2_gain, "fsdp", axis=0, tiled=True),
        lax.all_gather(norm2_bias, "fsdp", axis=0, tiled=True),
        lax.all_gather(up_weight, "fsdp", axis=0, tiled=True),
        lax.all_gather(up_bias, "fsdp", axis=0, tiled=True),
        lax.all_gather(down_weight, "fsdp", axis=0, tiled=True),
        lax.all_gather(down_bias, "fsdp", axis=0, tiled=True),
    )
    query_segment = lax.dynamic_slice_in_dim(segments, first_row, own_rows, 1)
    query_place = first_row + jnp.arange(own_rows, dtype=jnp.int32)
    key_place = jnp.arange(length, dtype=jnp.int32)
    visible = (query_segment[:, :, None] == segments[:, None, :]) & (
        key_place[None, None, :] <= query_place[None, :, None]
    )
    tokens_in = inputs.astype(jnp.float32).reshape(token_count, model_width)
    normed_one = layer_norm_core(
        tokens_in, gain_one.astype(jnp.float32), shift_one.astype(jnp.float32)
    ).astype(jnp.bfloat16)
    offsets = jnp.concatenate([query_shift, jnp.zeros_like(query_shift), value_shift]).astype(
        jnp.float32
    )
    projected = (
        jnp.dot(normed_one, qkv_full, preferred_element_type=jnp.float32) + offsets
    ).astype(jnp.bfloat16)
    projected = projected.reshape(seq_count, own_rows, 3 * model_width)
    queries = projected[:, :, :model_width]
    key_value = projected[:, :, model_width:]
    gathered_keys = lax.all_gather(key_value, "fsdp", axis=1, tiled=True)

    def attend_pair(pair_index):
        query_pair = pair_columns(queries, pair_index, 0)
        key_pair = pair_columns(gathered_keys, pair_index, 0)
        value_pair = pair_columns(gathered_keys, pair_index, model_width)
        raw_scores = jnp.einsum(
            "stgd,slgd->sgtl", query_pair, key_pair, preferred_element_type=jnp.float32
        )
        scores = jnp.where(visible[:, None], raw_scores * score_scale, -1e30)
        highest = jnp.max(scores, axis=-1, keepdims=True)
        weights = jnp.exp(scores - highest)
        denominator = jnp.sum(weights, axis=-1, keepdims=True)
        probability = (weights / denominator).astype(jnp.bfloat16)
        context = jnp.einsum(
            "sgtl,slgd->stgd", probability, value_pair, preferred_element_type=jnp.float32
        )
        return (
            context.reshape(seq_count, own_rows, 2 * HD),
            (highest + jnp.log(denominator))[..., 0],
        )

    contexts, logsums = lax.map(attend_pair, jnp.arange(pair_count))
    mixed = regroup(contexts).reshape(token_count, model_width).astype(jnp.bfloat16)
    attention_out = jnp.dot(
        mixed, proj_full, preferred_element_type=jnp.float32
    ) + proj_shift.astype(jnp.float32)
    residual = tokens_in + attention_out
    normed_two = layer_norm_core(
        residual, gain_two.astype(jnp.float32), shift_two.astype(jnp.float32)
    ).astype(jnp.bfloat16)
    upward = jnp.dot(normed_two, up_full, preferred_element_type=jnp.float32) + up_shift.astype(
        jnp.float32
    )
    activated = smooth_gate(upward).astype(jnp.bfloat16)
    downward = jnp.dot(
        activated, down_full, preferred_element_type=jnp.float32
    ) + down_shift.astype(jnp.float32)
    layer_out = (residual + downward).astype(jnp.bfloat16)
    back_gain_one, back_qkv, back_proj, back_gain_two, back_up, back_down = (
        lax.all_gather(norm1_gain, "fsdp", axis=0, tiled=True),
        lax.all_gather(qkv_weight, "fsdp", axis=0, tiled=True),
        lax.all_gather(proj_weight, "fsdp", axis=0, tiled=True),
        lax.all_gather(norm2_gain, "fsdp", axis=0, tiled=True),
        lax.all_gather(up_weight, "fsdp", axis=0, tiled=True),
        lax.all_gather(down_weight, "fsdp", axis=0, tiled=True),
    )
    upstream = cotangent.astype(jnp.float32).reshape(token_count, model_width)
    down_grad = cotangent.reshape(token_count, model_width)
    grad_down_weight = jnp.einsum(
        "nf,nd->fd", activated, down_grad, preferred_element_type=jnp.float32
    )
    grad_down_shift = jnp.sum(down_grad.astype(jnp.float32), axis=0)
    grad_activated = jnp.einsum(
        "nd,fd->nf", down_grad, back_down, preferred_element_type=jnp.float32
    )
    gate_value, gate_pullback = jax.vjp(smooth_gate, upward)
    up_grad = gate_pullback(grad_activated)[0].astype(jnp.bfloat16)
    grad_up_weight = jnp.einsum(
        "nd,nf->df", normed_two, up_grad, preferred_element_type=jnp.float32
    )
    grad_up_shift = jnp.sum(up_grad.astype(jnp.float32), axis=0)
    grad_normed_two = jnp.einsum("nf,df->nd", up_grad, back_up, preferred_element_type=jnp.float32)
    norm_value, norm_pullback = jax.vjp(
        layer_norm_core, residual, back_gain_two.astype(jnp.float32), shift_two.astype(jnp.float32)
    )
    grad_residual_norm, grad_gain_two, grad_shift_two = norm_pullback(grad_normed_two)
    grad_residual = upstream + grad_residual_norm
    attention_grad = grad_residual.astype(jnp.bfloat16)
    grad_proj_weight = jnp.einsum(
        "nd,ne->de", mixed, attention_grad, preferred_element_type=jnp.float32
    )
    grad_proj_shift = jnp.sum(attention_grad.astype(jnp.float32), axis=0)
    grad_mixed = jnp.einsum(
        "ne,de->nd", attention_grad, back_proj, preferred_element_type=jnp.float32
    )
    grad_mixed = grad_mixed.astype(jnp.bfloat16).reshape(seq_count, own_rows, model_width)

    def recompute(pair_index):
        query_pair = pair_columns(queries, pair_index, 0)
        key_pair = pair_columns(gathered_keys, pair_index, 0)
        value_pair = pair_columns(gathered_keys, pair_index, model_width)
        grad_context = pair_columns(grad_mixed, pair_index, 0)
        raw_scores = jnp.einsum(
            "stgd,slgd->sgtl", query_pair, key_pair, preferred_element_type=jnp.float32
        )
        scores = jnp.where(visible[:, None], raw_scores * score_scale, -1e30)
        probability = jnp.exp(scores - logsums[pair_index][..., None])
        grad_prob = jnp.einsum(
            "stgd,slgd->sgtl", grad_context, value_pair, preferred_element_type=jnp.float32
        )
        row_dots = jnp.sum(probability * grad_prob, axis=-1)
        grad_raw = (probability * (grad_prob - row_dots[..., None]) * score_scale).astype(
            jnp.bfloat16
        )
        grad_query = jnp.einsum(
            "sgtl,slgd->stgd", grad_raw, key_pair, preferred_element_type=jnp.float32
        )
        return (
            query_pair,
            probability,
            grad_context,
            grad_raw,
            grad_query.reshape(seq_count, own_rows, 2 * HD),
            row_dots,
        )

    def pair_grads(collected, pair_index):
        query_pair, probability, grad_context, grad_raw, grad_query, row_dots = recompute(
            pair_index
        )
        grad_key = jnp.einsum(
            "sgtl,stgd->slgd", grad_raw, query_pair, preferred_element_type=jnp.float32
        )
        grad_value = jnp.einsum(
            "sgtl,stgd->slgd",
            probability.astype(jnp.bfloat16),
            grad_context,
            preferred_element_type=jnp.float32,
        )
        start_col = pair_index * 2 * HD
        collected = lax.dynamic_update_slice_in_dim(
            collected, grad_key.reshape(seq_count, length, 2 * HD), start_col, 2
        )
        collected = lax.dynamic_update_slice_in_dim(
            collected, grad_value.reshape(seq_count, length, 2 * HD), model_width + start_col, 2
        )
        return (collected, grad_query)

    empty_grads = jnp.zeros((seq_count, length, 2 * model_width), jnp.float32)
    partial_keyval, grad_queries = lax.scan(pair_grads, empty_grads, jnp.arange(pair_count))
    grad_keyval = lax.psum_scatter(
        partial_keyval.astype(jnp.bfloat16), "fsdp", scatter_dimension=1, tiled=True
    ).astype(jnp.float32)
    qkv_grad = jnp.concatenate([regroup(grad_queries), grad_keyval], axis=2).astype(jnp.bfloat16)
    qkv_grad = qkv_grad.reshape(token_count, 3 * model_width)
    grad_qkv_weight = jnp.einsum(
        "nd,ne->de", normed_one, qkv_grad, preferred_element_type=jnp.float32
    )
    column_sums = jnp.sum(qkv_grad.astype(jnp.float32), axis=0)
    grad_query_shift = column_sums[:model_width]
    grad_value_shift = column_sums[2 * model_width :]
    grad_normed_one = jnp.einsum(
        "ne,de->nd", qkv_grad, back_qkv, preferred_element_type=jnp.float32
    )
    first_value, first_pullback = jax.vjp(
        layer_norm_core, tokens_in, back_gain_one.astype(jnp.float32), shift_one.astype(jnp.float32)
    )
    grad_input_norm, grad_gain_one, grad_shift_one = first_pullback(grad_normed_one)
    input_grad = grad_residual + grad_input_norm
    (
        own_gain_one,
        own_shift_one,
        own_qkv,
        own_query,
        own_value,
        own_proj,
        own_proj_shift,
        own_gain_two,
        own_shift_two,
        own_up,
        own_up_shift,
        own_down,
        own_down_shift,
    ) = (
        lax.psum_scatter(grad_gain_one, "fsdp", scatter_dimension=0, tiled=True),
        lax.psum_scatter(grad_shift_one, "fsdp", scatter_dimension=0, tiled=True),
        lax.psum_scatter(grad_qkv_weight, "fsdp", scatter_dimension=0, tiled=True),
        lax.psum_scatter(grad_query_shift, "fsdp", scatter_dimension=0, tiled=True),
        lax.psum_scatter(grad_value_shift, "fsdp", scatter_dimension=0, tiled=True),
        lax.psum_scatter(grad_proj_weight, "fsdp", scatter_dimension=0, tiled=True),
        lax.psum_scatter(grad_proj_shift, "fsdp", scatter_dimension=0, tiled=True),
        lax.psum_scatter(grad_gain_two, "fsdp", scatter_dimension=0, tiled=True),
        lax.psum_scatter(grad_shift_two, "fsdp", scatter_dimension=0, tiled=True),
        lax.psum_scatter(grad_up_weight, "fsdp", scatter_dimension=0, tiled=True),
        lax.psum_scatter(grad_up_shift, "fsdp", scatter_dimension=0, tiled=True),
        lax.psum_scatter(grad_down_weight, "fsdp", scatter_dimension=0, tiled=True),
        lax.psum_scatter(grad_down_shift, "fsdp", scatter_dimension=0, tiled=True),
    )
    (
        sum_gain_one,
        sum_shift_one,
        sum_qkv,
        sum_query,
        sum_value,
        sum_proj,
        sum_proj_shift,
        sum_gain_two,
        sum_shift_two,
        sum_up,
        sum_up_shift,
        sum_down,
        sum_down_shift,
    ) = lax.psum(
        (
            own_gain_one,
            own_shift_one,
            own_qkv,
            own_query,
            own_value,
            own_proj,
            own_proj_shift,
            own_gain_two,
            own_shift_two,
            own_up,
            own_up_shift,
            own_down,
            own_down_shift,
        ),
        "dp",
    )
    return (
        layer_out.reshape(seq_count, own_rows, model_width),
        input_grad.reshape(seq_count, own_rows, model_width),
        sum_gain_one,
        sum_shift_one,
        sum_qkv,
        sum_query,
        sum_value,
        sum_proj,
        sum_proj_shift,
        sum_gain_two,
        sum_shift_two,
        sum_up,
        sum_up_shift,
        sum_down,
        sum_down_shift,
    )


def solution(mesh):
    in_specs = (
        P("dp", "fsdp", None),
        P("dp", "fsdp", None),
        P("dp", None),
        P("fsdp"),
        P("fsdp"),
        P("fsdp", None),
        P("fsdp"),
        P("fsdp"),
        P("fsdp", None),
        P("fsdp"),
        P("fsdp"),
        P("fsdp"),
        P("fsdp", None),
        P("fsdp"),
        P("fsdp", None),
        P("fsdp"),
    )
    out_specs = (
        P("dp", "fsdp", None),
        P("dp", "fsdp", None),
        P("fsdp"),
        P("fsdp"),
        P("fsdp", None),
        P("fsdp"),
        P("fsdp"),
        P("fsdp", None),
        P("fsdp"),
        P("fsdp"),
        P("fsdp"),
        P("fsdp", None),
        P("fsdp"),
        P("fsdp", None),
        P("fsdp"),
    )
    return jax.shard_map(local, mesh=mesh, in_specs=in_specs, out_specs=out_specs, check_vma=False)
```

profile of v0, /device:TPU:0, one launch (start us, length us, event | category | flops | bytes accessed | tf_op | source)
XLA Modules:
  0.0 1656.0 jit_solution(7502779590632231843)
XLA Ops:
  16.7 26.0 %all-reduce.20 = (bf16[768]{0:T(1024)(128)(2,1)S(1)}, bf16[768]{0:T(1024)(128)(2,1)S(1)}, bf16[768]{0:T(1024)(128)(2,1)S(1)}, bf16[768]{0:T(1024)(128)(2,1)S(1)}...) all-reduce(bf16[768]{0:T(1024)(128)(2,1)S(1)} %dynamic-update-slice, ...), channel_id=1, replica_groups=mesh['fsdp'=8,'dp'=4] {'fsdp'}, use_global_device_ids=true, to_apply=%add.1 | all-reduce | flops 6144 | bytes 24576
  61.8 8.9 all-gather
  75.6 112.8 %all-gather.9.cloned.1.call-done = bf16[4,2048,1536]{1,2,0:T(8,128)(2,1)} async-done(((bf16[4,256,1536]{1,2,0:T(8,128)(2,1)}), bf16[4,2048,1536]{1,2,0:T(8,128)(2,1)}) %all-gather.9.cloned.1.call-update) | async-done | bytes 25165840 | tf_op jit(solution)/shard_map/all_gather | solution.py:103
  189.7 162.5 %while.30 = (s32[]{:T(128)}, bf16[6,4,256,128]{2,3,1,0:T(8,128)(2,1)}, f32[6,4,2,256]{3,2,1,0:T(2,128)}, s32[6]{0:T(128)S(1)}, bf16[4,2048,1536]{1,2,0:T(8,128)(...) while((s32[]{:T(128)}, ...), condition=%wide.region_5.6_spmd.clone, body=%wide.region_2.5_spmd.clone.sunk | while | flops 1128265728 | bytes 73502992 | solution.py:125
  362.2 11.4 fusion.78
  373.6 15.5 convert_reduce_fusion
  389.1 10.8 multiply_reduce_fusion.1
  406.5 8.5 broadcast_in_dim.99
  414.9 624.8 %while.31 = (s32[]{:T(128)}, bf16[4,2048,1536]{1,2,0:T(8,128)(2,1)}, bf16[6,4,256,128]{2,3,1,0:T(8,128)(2,1)}, s32[6]{0:T(128)S(1)}, bf16[4,256,768]{1,2,0:T(8,1...) while((s32[]{:T(128)}, ...), condition=%wide.region_12.13_spmd.clone, body=%wide.region_10.12_spmd.clone.sunk | while | flops 2797608960 | bytes 186462688 | solution.py:233
  426.3 8.2 fusion.154
  434.5 8.1 fusion.155
  442.6 30.8 %fusion.158 = bf16[4,2,64,256]{3,2,1,0:T(8,128)(2,1)S(1)} fusion(bf16[4,2048,2,64]{1,3,2,0:T(8,128)(2,1)S(1)} %bitcast.170, f32[4,2,256,2048]{3,2,1,0:T(8,128)} %fusion.154, f32[4,2,256,2048]{3,2,1,0:T(8,128)} %fusion.155, f32[4,2,256]{2,1,0:T(2,128)S(1)} %dynamic-slice_bitcast_fusion.2, pred[4,256,2048]{2,1,0:T(8,128)(4,1)} %compare_and_fusion.5), kind=kOutput, calls=%fused_computation.22.clone.1 | convolution fusion | flops 583012352 | bytes 38019072 | tf_op jit(solution)/shard_map/while/body/eval_jaxpr/sgtl,slgd->stgd/dot_general | solution.py:198
  473.4 33.0 %fusion.156 = bf16[4,2,64,2048]{3,2,1,0:T(8,128)(2,1)} fusion(bf16[4,256,2,64]{1,3,2,0:T(8,128)(2,1)S(1)} %bitcast.176, f32[4,2,256,2048]{3,2,1,0:T(8,128)} %fusion.154, f32[4,2,256,2048]{3,2,1,0:T(8,128)} %fusion.155, f32[4,2,256]{2,1,0:T(2,128)S(1)} %dynamic-slice_bitcast_fusion.2, pred[4,256,2048]{2,1,0:T(8,128)(4,1)} %compare_and_fusion.5), kind=kOutput, calls=%fused_computation.23.clone.1 | convolution fusion | flops 583012352 | bytes 38019072 | tf_op jit(solution)/shard_map/while/body/eval_jaxpr/sgtl,stgd->slgd/dot_general | solution.py:214
  506.4 8.5 fusion.157
  530.3 8.2 fusion.154
  546.6 30.8 %fusion.158 = bf16[4,2,64,256]{3,2,1,0:T(8,128)(2,1)S(1)} fusion(bf16[4,2048,2,64]{1,3,2,0:T(8,128)(2,1)S(1)} %bitcast.170, f32[4,2,256,2048]{3,2,1,0:T(8,128)} %fusion.154, f32[4,2,256,2048]{3,2,1,0:T(8,128)} %fusion.155, f32[4,2,256]{2,1,0:T(2,128)S(1)} %dynamic-slice_bitcast_fusion.2, pred[4,256,2048]{2,1,0:T(8,128)(4,1)} %compare_and_fusion.5), kind=kOutput, calls=%fused_computation.22.clone.1 | convolution fusion | flops 583012352 | bytes 38019072 | tf_op jit(solution)/shard_map/while/body/eval_jaxpr/sgtl,slgd->stgd/dot_general | solution.py:198
  577.4 33.0 %fusion.156 = bf16[4,2,64,2048]{3,2,1,0:T(8,128)(2,1)} fusion(bf16[4,256,2,64]{1,3,2,0:T(8,128)(2,1)S(1)} %bitcast.176, f32[4,2,256,2048]{3,2,1,0:T(8,128)} %fusion.154, f32[4,2,256,2048]{3,2,1,0:T(8,128)} %fusion.155, f32[4,2,256]{2,1,0:T(2,128)S(1)} %dynamic-slice_bitcast_fusion.2, pred[4,256,2048]{2,1,0:T(8,128)(4,1)} %compare_and_fusion.5), kind=kOutput, calls=%fused_computation.23.clone.1 | convolution fusion | flops 583012352 | bytes 38019072 | tf_op jit(solution)/shard_map/while/body/eval_jaxpr/sgtl,stgd->slgd/dot_general | solution.py:214
  610.4 8.5 fusion.157
  634.3 8.2 fusion.154
  642.5 8.1 fusion.155
  650.6 30.8 %fusion.158 = bf16[4,2,64,256]{3,2,1,0:T(8,128)(2,1)S(1)} fusion(bf16[4,2048,2,64]{1,3,2,0:T(8,128)(2,1)S(1)} %bitcast.170, f32[4,2,256,2048]{3,2,1,0:T(8,128)} %fusion.154, f32[4,2,256,2048]{3,2,1,0:T(8,128)} %fusion.155, f32[4,2,256]{2,1,0:T(2,128)S(1)} %dynamic-slice_bitcast_fusion.2, pred[4,256,2048]{2,1,0:T(8,128)(4,1)} %compare_and_fusion.5), kind=kOutput, calls=%fused_computation.22.clone.1 | convolution fusion | flops 583012352 | bytes 38019072 | tf_op jit(solution)/shard_map/while/body/eval_jaxpr/sgtl,slgd->stgd/dot_general | solution.py:198
  681.4 33.0 %fusion.156 = bf16[4,2,64,2048]{3,2,1,0:T(8,128)(2,1)} fusion(bf16[4,256,2,64]{1,3,2,0:T(8,128)(2,1)S(1)} %bitcast.176, f32[4,2,256,2048]{3,2,1,0:T(8,128)} %fusion.154, f32[4,2,256,2048]{3,2,1,0:T(8,128)} %fusion.155, f32[4,2,256]{2,1,0:T(2,128)S(1)} %dynamic-slice_bitcast_fusion.2, pred[4,256,2048]{2,1,0:T(8,128)(4,1)} %compare_and_fusion.5), kind=kOutput, calls=%fused_computation.23.clone.1 | convolution fusion | flops 583012352 | bytes 38019072 | tf_op jit(solution)/shard_map/while/body/eval_jaxpr/sgtl,stgd->slgd/dot_general | solution.py:214
  714.4 8.5 fusion.157
  738.3 8.2 fusion.154
  754.6 30.8 %fusion.158 = bf16[4,2,64,256]{3,2,1,0:T(8,128)(2,1)S(1)} fusion(bf16[4,2048,2,64]{1,3,2,0:T(8,128)(2,1)S(1)} %bitcast.170, f32[4,2,256,2048]{3,2,1,0:T(8,128)} %fusion.154, f32[4,2,256,2048]{3,2,1,0:T(8,128)} %fusion.155, f32[4,2,256]{2,1,0:T(2,128)S(1)} %dynamic-slice_bitcast_fusion.2, pred[4,256,2048]{2,1,0:T(8,128)(4,1)} %compare_and_fusion.5), kind=kOutput, calls=%fused_computation.22.clone.1 | convolution fusion | flops 583012352 | bytes 38019072 | tf_op jit(solution)/shard_map/while/body/eval_jaxpr/sgtl,slgd->stgd/dot_general | solution.py:198
  785.4 33.0 %fusion.156 = bf16[4,2,64,2048]{3,2,1,0:T(8,128)(2,1)} fusion(bf16[4,256,2,64]{1,3,2,0:T(8,128)(2,1)S(1)} %bitcast.176, f32[4,2,256,2048]{3,2,1,0:T(8,128)} %fusion.154, f32[4,2,256,2048]{3,2,1,0:T(8,128)} %fusion.155, f32[4,2,256]{2,1,0:T(2,128)S(1)} %dynamic-slice_bitcast_fusion.2, pred[4,256,2048]{2,1,0:T(8,128)(4,1)} %compare_and_fusion.5), kind=kOutput, calls=%fused_computation.23.clone.1 | convolution fusion | flops 583012352 | bytes 38019072 | tf_op jit(solution)/shard_map/while/body/eval_jaxpr/sgtl,stgd->slgd/dot_general | solution.py:214
  818.5 8.5 fusion.157
  842.4 8.2 fusion.154
  858.7 30.8 %fusion.158 = bf16[4,2,64,256]{3,2,1,0:T(8,128)(2,1)S(1)} fusion(bf16[4,2048,2,64]{1,3,2,0:T(8,128)(2,1)S(1)} %bitcast.170, f32[4,2,256,2048]{3,2,1,0:T(8,128)} %fusion.154, f32[4,2,256,2048]{3,2,1,0:T(8,128)} %fusion.155, f32[4,2,256]{2,1,0:T(2,128)S(1)} %dynamic-slice_bitcast_fusion.2, pred[4,256,2048]{2,1,0:T(8,128)(4,1)} %compare_and_fusion.5), kind=kOutput, calls=%fused_computation.22.clone.1 | convolution fusion | flops 583012352 | bytes 38019072 | tf_op jit(solution)/shard_map/while/body/eval_jaxpr/sgtl,slgd->stgd/dot_general | solution.py:198
  889.5 33.0 %fusion.156 = bf16[4,2,64,2048]{3,2,1,0:T(8,128)(2,1)} fusion(bf16[4,256,2,64]{1,3,2,0:T(8,128)(2,1)S(1)} %bitcast.176, f32[4,2,256,2048]{3,2,1,0:T(8,128)} %fusion.154, f32[4,2,256,2048]{3,2,1,0:T(8,128)} %fusion.155, f32[4,2,256]{2,1,0:T(2,128)S(1)} %dynamic-slice_bitcast_fusion.2, pred[4,256,2048]{2,1,0:T(8,128)(4,1)} %compare_and_fusion.5), kind=kOutput, calls=%fused_computation.23.clone.1 | convolution fusion | flops 583012352 | bytes 38019072 | tf_op jit(solution)/shard_map/while/body/eval_jaxpr/sgtl,stgd->slgd/dot_general | solution.py:214
  922.5 8.5 fusion.157
  946.4 8.2 fusion.154
  962.7 30.8 %fusion.158 = bf16[4,2,64,256]{3,2,1,0:T(8,128)(2,1)S(1)} fusion(bf16[4,2048,2,64]{1,3,2,0:T(8,128)(2,1)S(1)} %bitcast.170, f32[4,2,256,2048]{3,2,1,0:T(8,128)} %fusion.154, f32[4,2,256,2048]{3,2,1,0:T(8,128)} %fusion.155, f32[4,2,256]{2,1,0:T(2,128)S(1)} %dynamic-slice_bitcast_fusion.2, pred[4,256,2048]{2,1,0:T(8,128)(4,1)} %compare_and_fusion.5), kind=kOutput, calls=%fused_computation.22.clone.1 | convolution fusion | flops 583012352 | bytes 38019072 | tf_op jit(solution)/shard_map/while/body/eval_jaxpr/sgtl,slgd->stgd/dot_general | solution.py:198
  993.5 33.0 %fusion.156 = bf16[4,2,64,2048]{3,2,1,0:T(8,128)(2,1)} fusion(bf16[4,256,2,64]{1,3,2,0:T(8,128)(2,1)S(1)} %bitcast.176, f32[4,2,256,2048]{3,2,1,0:T(8,128)} %fusion.154, f32[4,2,256,2048]{3,2,1,0:T(8,128)} %fusion.155, f32[4,2,256]{2,1,0:T(2,128)S(1)} %dynamic-slice_bitcast_fusion.2, pred[4,256,2048]{2,1,0:T(8,128)(4,1)} %compare_and_fusion.5), kind=kOutput, calls=%fused_computation.23.clone.1 | convolution fusion | flops 583012352 | bytes 38019072 | tf_op jit(solution)/shard_map/while/body/eval_jaxpr/sgtl,stgd->slgd/dot_general | solution.py:214
  1026.5 8.5 fusion.157
  1039.7 32.7 %copy.46 = bf16[4,2048,1536]{2,1,0:T(8,128)(2,1)} copy(bf16[4,2048,1536]{1,2,0:T(8,128)(2,1)} %get-tuple-element.224) | data formatting | bytes 50331648 | tf_op jit(solution)/shard_map/while | solution.py:233
  1077.5 11.8 fusion.77
  1091.1 14.4 fusion.79
  1111.5 117.8 %reduce-scatter.6.cloned.1.call-done = bf16[4,256,1536]{2,1,0:T(8,128)(2,1)} async-done(((bf16[4,2048,1536]{2,1,0:T(8,128)(2,1)}), bf16[4,256,1536]{2,1,0:T(8,128)(2,1)}) %reduce-scatter.6.cloned.1.call-update) | async-done | bytes 3145744 | tf_op jit(solution)/shard_map/reduce_scatter | solution.py:234
  1229.3 9.1 fusion.69
  1240.1 35.1 %reduce-scatter.10.cloned.1.call-done = f32[96,768]{1,0:T(8,128)} async-done(((f32[768,768]{1,0:T(8,128)}), f32[96,768]{1,0:T(8,128)}) %reduce-scatter.10.cloned.1.call-update) | async-done | bytes 294928 | tf_op jit(solution)/shard_map/reduce_scatter | solution.py:273
  1275.2 80.4 %reduce-scatter.12.cloned.1.call-done = f32[96,3072]{1,0:T(8,128)} async-done(((f32[768,3072]{1,0:T(8,128)}), f32[96,3072]{1,0:T(8,128)}) %reduce-scatter.12.cloned.1.call-update) | async-done | bytes 1179664 | tf_op jit(solution)/shard_map/reduce_scatter | solution.py:277
  1355.6 80.4 %reduce-scatter.14.cloned.1.call-done = f32[384,768]{1,0:T(8,128)} async-done(((f32[3072,768]{1,0:T(8,128)}), f32[384,768]{1,0:T(8,128)}) %reduce-scatter.14.cloned.1.call-update) | async-done | bytes 1179664 | tf_op jit(solution)/shard_map/reduce_scatter | solution.py:279
  1436.0 69.3 %reduce-scatter.8.cloned.1.call-done = f32[96,2304]{1,0:T(8,128)} async-done(((f32[768,2304]{1,0:T(8,128)}), f32[96,2304]{1,0:T(8,128)}) %reduce-scatter.8.cloned.1.call-update) | async-done | bytes 884752 | tf_op jit(solution)/shard_map/reduce_scatter | solution.py:270
  1505.4 13.7 add_convert_fusion.1
  1525.9 25.1 %all-reduce.17 = (f32[768]{0:T(1024)S(1)}, f32[768]{0:T(1024)S(1)}, f32[768]{0:T(1024)S(1)}, f32[768]{0:T(1024)S(1)}, f32[768]{0:T(1024)S(1)}, /*index=5*/f32[76...) all-reduce(f32[768]{0:T(1024)S(1)} %get-tuple-element.310, ...), channel_id=3, replica_groups=mesh['fsdp'=8,'dp'=4] {'fsdp'}, use_global_device_ids=true, to_apply=%region_17.18.clone | all-reduce | flops 9216 | bytes 73728
  1551.7 13.4 all-reduce.18
  1569.8 73.4 %all-reduce.23.cloned.1.call-done = (f32[96,2304]{1,0:T(8,128)}, f32[96,768]{1,0:T(8,128)}, f32[96,3072]{1,0:T(8,128)}, f32[384,768]{1,0:T(8,128)}) async-done(((f32[96,2304]{1,0:T(8,128)}, f32[96,768]{1,0:T(8,128)}, f32[96,3072]{1,0:T(8,128)}, f32[384,768]{1,0:T(8,128)}), (f32[96,2304]{1,0:T(8,128)}, f32[96,768]{1,0:T(8,128)}, f32[96,3072]{1,0:T(8,128)}, ...) | async-done | bytes 3538960 | tf_op jit(solution)/shard_map/psum | solution.py:296
  (373 shorter events, 348.8 us)
Async XLA Ops:
  7.2 37.2 %copy-start.2 = (bf16[4,256,768]{2,1,0:T(8,128)(2,1)S(1)}, bf16[4,256,768]{2,1,0:T(8,128)(2,1)}, u32[]{:S(2)}) copy-start(bf16[4,256,768]{2,1,0:T(8,128)(2,1)} %param.20) | copy-start | bytes 4718596
  7.2 39.6 %all-gather.7.cloned.1.call-start = ((), (), s32[]{:S(2)}) async-start(), calls=%async_computation.5 | async-start | bytes 3981312 | tf_op jit(solution)/shard_map/all_gather | solution.py:72
  7.9 180.5 %all-gather.9.cloned.1.call-start = ((), (), s32[]{:S(2)}) async-start(), calls=%async_computation.6 | async-start | bytes 28311552 | tf_op jit(solution)/shard_map/all_gather | solution.py:103
  46.3 6.6 copy-start.18
  58.0 298.4 %all-gather.11.cloned.1.call-start = ((), (), s32[]{:S(2)}) async-start(), calls=%async_computation.7 | async-start | bytes 1327104 | tf_op jit(solution)/shard_map/all_gather | solution.py:75
  58.8 303.4 %all-gather.13.cloned.1.call-start = ((), (), s32[]{:S(2)}) async-start(), calls=%async_computation.8 | async-start | bytes 5308416 | tf_op jit(solution)/shard_map/all_gather | solution.py:79
  59.4 314.3 %all-gather.15.cloned.1.call-start = ((), (), s32[]{:S(2)}) async-start(), calls=%async_computation.9 | async-start | bytes 5308416 | tf_op jit(solution)/shard_map/all_gather | solution.py:81
  60.0 1169.4 %reduce-scatter.6.cloned.1.call-start = ((), (), s32[]{:S(2)}) async-start(), calls=%async_computation.10 | async-start | bytes 28311552 | tf_op jit(solution)/shard_map/reduce_scatter | solution.py:234
  360.0 40.0 %copy-start.24 = (f32[1024]{0:T(1024)}, f32[1024]{0:T(1024)S(1)}, u32[]{:S(2)}) copy-start(f32[1024]{0:T(1024)S(1)} %broadcast_multiply_fusion) | copy-start | bytes 12292
  362.1 37.9 %copy-start.26 = (f32[1024]{0:T(1024)}, f32[1024]{0:T(1024)S(1)}, u32[]{:S(2)}) copy-start(f32[1024]{0:T(1024)S(1)} %fusion.72) | copy-start | bytes 12292
  362.1 11.5 copy-start.9
  362.1 11.5 copy-start.43
  373.6 15.5 copy-start.6
  389.1 10.8 copy-start.12
  415.1 5.2 copy-start.22
  473.4 33.0 %copy-start = (pred[4,256,2048]{2,1,0:T(8,128)(4,1)S(1)}, pred[4,256,2048]{2,1,0:T(8,128)(4,1)}, u32[]{:S(2)}) copy-start(pred[4,256,2048]{2,1,0:T(8,128)(4,1)} %compare_and_fusion.5) | copy-start | bytes 6291460 | tf_op jit(solution)/shard_map/while
  506.4 9.2 copy-start.1
  519.1 5.2 copy-start.22
  577.4 33.0 %copy-start = (pred[4,256,2048]{2,1,0:T(8,128)(4,1)S(1)}, pred[4,256,2048]{2,1,0:T(8,128)(4,1)}, u32[]{:S(2)}) copy-start(pred[4,256,2048]{2,1,0:T(8,128)(4,1)} %compare_and_fusion.5) | copy-start | bytes 6291460 | tf_op jit(solution)/shard_map/while
  610.4 9.2 copy-start.1
  623.2 5.2 copy-start.22
  681.4 33.0 %copy-start = (pred[4,256,2048]{2,1,0:T(8,128)(4,1)S(1)}, pred[4,256,2048]{2,1,0:T(8,128)(4,1)}, u32[]{:S(2)}) copy-start(pred[4,256,2048]{2,1,0:T(8,128)(4,1)} %compare_and_fusion.5) | copy-start | bytes 6291460 | tf_op jit(solution)/shard_map/while
  714.4 9.2 copy-start.1
  727.2 5.2 copy-start.22
  785.4 33.0 %copy-start = (pred[4,256,2048]{2,1,0:T(8,128)(4,1)S(1)}, pred[4,256,2048]{2,1,0:T(8,128)(4,1)}, u32[]{:S(2)}) copy-start(pred[4,256,2048]{2,1,0:T(8,128)(4,1)} %compare_and_fusion.5) | copy-start | bytes 6291460 | tf_op jit(solution)/shard_map/while
  818.5 9.2 copy-start.1
  831.3 5.2 copy-start.22
  889.5 33.0 %copy-start = (pred[4,256,2048]{2,1,0:T(8,128)(4,1)S(1)}, pred[4,256,2048]{2,1,0:T(8,128)(4,1)}, u32[]{:S(2)}) copy-start(pred[4,256,2048]{2,1,0:T(8,128)(4,1)} %compare_and_fusion.5) | copy-start | bytes 6291460 | tf_op jit(solution)/shard_map/while
  922.5 9.2 copy-start.1
  935.2 5.2 copy-start.22
  993.5 33.0 %copy-start = (pred[4,256,2048]{2,1,0:T(8,128)(4,1)S(1)}, pred[4,256,2048]{2,1,0:T(8,128)(4,1)}, u32[]{:S(2)}) copy-start(pred[4,256,2048]{2,1,0:T(8,128)(4,1)} %compare_and_fusion.5) | copy-start | bytes 6291460 | tf_op jit(solution)/shard_map/while
  1026.5 9.2 copy-start.1
  1072.4 5.0 copy-start.7
  1072.5 5.0 copy-start.25
  1072.5 202.7 %reduce-scatter.10.cloned.1.call-start = ((), (), s32[]{:S(2)}) async-start(), calls=%async_computation.12 | async-start | bytes 2654208 | tf_op jit(solution)/shard_map/reduce_scatter | solution.py:273
  1077.4 278.2 %reduce-scatter.12.cloned.1.call-start = ((), (), s32[]{:S(2)}) async-start(), calls=%async_computation.13 | async-start | bytes 10616832 | tf_op jit(solution)/shard_map/reduce_scatter | solution.py:277
  1089.3 346.7 %reduce-scatter.14.cloned.1.call-start = ((), (), s32[]{:S(2)}) async-start(), calls=%async_computation.14 | async-start | bytes 10616832 | tf_op jit(solution)/shard_map/reduce_scatter | solution.py:279
  1105.6 399.8 %reduce-scatter.8.cloned.1.call-start = ((), (), s32[]{:S(2)}) async-start(), calls=%async_computation.11 | async-start | bytes 7962624 | tf_op jit(solution)/shard_map/reduce_scatter | solution.py:270
  1111.5 126.9 %copy-start.13 = (bf16[128,8,6,128]{3,1,2,0:T(8,128)(2,1)}, bf16[128,8,6,128]{3,1,2,0:T(8,128)(2,1)S(1)}, u32[]{:S(2)}) copy-start(bf16[128,8,6,128]{3,1,2,0:T(8,128)(2,1)S(1)} %copy.58) | copy-start | bytes 4718596
  1238.5 404.8 %all-reduce.23.cloned.1.call-start = ((), (), s32[]{:S(2)}) async-start(), calls=%async_computation.15 | async-start | bytes 7077888 | tf_op jit(solution)/shard_map/psum | solution.py:296
  1505.3 13.8 copy-start.4
  1505.4 13.8 copy-start.14
  1505.4 13.8 copy-start.17
  1505.4 13.8 copy-start.31
  1505.4 13.8 copy-start.33
  1505.4 13.8 copy-start.51
  1524.1 41.0 %copy-start.39 = (f32[1024]{0:T(1024)S(1)}, f32[1024]{0:T(1024)}, u32[]{:S(2)}) copy-start(f32[1024]{0:T(1024)} %copy-done.38) | copy-start | bytes 12292
  1643.3 5.0 copy-start.20
  (36 other events, 83.2 us)
Sparse Core Ops, SparseCore 0:
  9.9 36.8 all-gather.6
  58.2 130.2 all-gather.8
  190.3 24.0 all-gather.10
  216.2 38.9 all-gather.12
  256.8 38.9 all-gather.14
  1072.6 156.7 reduce-scatter.5
  1232.7 42.4 reduce-scatter.9
  1279.1 76.4 reduce-scatter.11
  1359.5 76.4 reduce-scatter.13
  1439.8 65.4 reduce-scatter.7
  1508.0 135.2 all-reduce.22
where the time goes:
time: 1660 us
  matrix products  704 us (42%)
  waiting for transfers between devices  572 us (34%)
  local copies, waits for them, and re-layouts  184 us (11%)
  other arithmetic  85 us (5%)
  blocking collectives  73.5 us (4%)
  loops' own time  20.7 us (1%)
  between operations  16.8 us (1%)
    dot_general x6, matrix products, pair_grads(): jnp.einsum('sgtl,stgd->slgd', grad_raw, query_pair, preferred_element_typ...  198 us
    dot_general x6, matrix products, recompute(): jnp.einsum('sgtl,slgd->stgd', grad_raw, key_pair, preferred_element_type=...  185 us
    reduce_scatter x1, waiting for transfers between devices, local(): lax.psum_scatter(partial_keyval.astype(jnp.bfloat16), 'fsdp', scatter_dim...  118 us
    all_gather x1, waiting for transfers between devices, local(): gathered_keys = lax.all_gather(key_value, 'fsdp', axis=1, tiled=True)  113 us
    reduce_scatter x1, waiting for transfers between devices, local(): lax.psum_scatter(grad_down_weight, 'fsdp', scatter_dimension=0, tiled=True)  80.4 us
    reduce_scatter x1, waiting for transfers between devices, local(): lax.psum_scatter(grad_up_weight, 'fsdp', scatter_dimension=0, tiled=True)  80.4 us
    psum x1, waiting for transfers between devices, local(): lax.psum((own_gain_one, own_shift_one, own_qkv, own_query, own_value, own...  73.4 us
    reduce_scatter x1, waiting for transfers between devices, local(): lax.psum_scatter(grad_qkv_weight, 'fsdp', scatter_dimension=0, tiled=True)  69.3 us
  transfers between devices with their start and end apart: 11, of which 8 were waited for; matrix products, arithmetic and copies ran while one was open for 16% of the time, Pallas kernels for 0%

commit v1 on v0

v1 whole, which is shorter than its diff:
```python
from functools import partial

import jax
import jax.numpy as jnp
from jax import lax
from jax.experimental import pallas as pl
from jax.experimental.pallas import tpu as pltpu
from jax.sharding import PartitionSpec as P

HD = 64
PAIR = 2 * HD
FWD_BLOCK = 512
BWD_BLOCK = 512
HIDDEN = -1e30
NT = (((1,), (1,)), ((), ()))


def layer_norm_core(values, gains, shifts):
    centre = jnp.mean(values, axis=-1, keepdims=True)
    centred = values - centre
    spread = jnp.mean(centred * centred, axis=-1, keepdims=True)
    return centred * lax.rsqrt(spread + 1e-05) * gains + shifts


def smooth_gate(values):
    return jax.nn.gelu(values, approximate=True)


def head_masks(block):
    first = lax.broadcasted_iota(jnp.int32, block.shape, 1) < HD
    zero = jnp.zeros_like(block)
    return jnp.where(first, block, zero), jnp.where(first, zero, block)


def attend_kernel(size, start_ref, query_ref, key_ref, value_ref, context_ref, logsum_ref):
    row_block = pl.program_id(1)
    scaled = query_ref[...] * jnp.asarray(HD ** (-0.5), jnp.bfloat16)
    query_heads = head_masks(scaled)
    starts = start_ref[...]
    lane_first = lax.broadcasted_iota(jnp.int32, (size, PAIR), 1) < HD
    columns = lax.broadcasted_iota(jnp.int32, (size, size), 1)

    def step(block, carry, diagonal):
        begin = pl.multiple_of(block * size, size)
        keys = key_ref[pl.ds(begin, size), :]
        values = value_ref[pl.ds(begin, size), :]
        one = jnp.ones_like(values)
        value_heads = (
            jnp.where(lane_first, values, one),
            jnp.where(lane_first, one, values),
        )
        seen = columns >= starts - begin
        if diagonal:
            seen = seen & (columns <= lax.broadcasted_iota(jnp.int32, (size, size), 0))
        out = []
        for head in range(2):
            highest, total = carry[head]
            scores = lax.dot_general(
                query_heads[head], keys, NT, preferred_element_type=jnp.float32
            )
            scores = jnp.where(seen, scores, HIDDEN)
            now = jnp.maximum(highest, jnp.max(scores, axis=1, keepdims=True))
            weights = jnp.exp(scores - now).astype(jnp.bfloat16)
            total = total * jnp.exp(highest - now) + jnp.dot(
                weights, value_heads[head], preferred_element_type=jnp.float32
            )
            out.append((now, total))
        return tuple(out)

    fresh = (jnp.full((size, 1), HIDDEN, jnp.float32), jnp.zeros((size, PAIR), jnp.float32))
    carry = lax.fori_loop(0, row_block, lambda b, c: step(b, c, False), (fresh, fresh))
    (high_a, total_a), (high_b, total_b) = step(row_block, carry, True)
    sum_a = total_a[:, HD : HD + 1]
    sum_b = total_b[:, 0:1]
    context_ref[...] = jnp.where(lane_first, total_a / sum_a, total_b / sum_b).astype(
        context_ref.dtype
    )
    logsum_ref[...] = jnp.where(lane_first, high_a + jnp.log(sum_a), high_b + jnp.log(sum_b))


def attend(received, starts, pairs):
    length = received.shape[0]
    size = min(FWD_BLOCK, length)
    whole = lambda third: pl.BlockSpec((length, PAIR), lambda p, r, t=third: (0, t * pairs + p))
    block = pl.BlockSpec((size, PAIR), lambda p, r: (r, p))
    pair_work = length * length * PAIR * 4
    return pl.pallas_call(
        partial(attend_kernel, size),
        grid=(pairs, length // size),
        in_specs=[pl.BlockSpec((size, 1), lambda p, r: (r, 0)), block, whole(1), whole(2)],
        out_specs=[block, block],
        out_shape=[
            jax.ShapeDtypeStruct((length, pairs * PAIR), jnp.bfloat16),
            jax.ShapeDtypeStruct((length, pairs * PAIR), jnp.float32),
        ],
        cost_estimate=pl.CostEstimate(
            flops=pairs * pair_work * 4,
            bytes_accessed=received.size * 4,
            transcendentals=pairs * length * length,
        ),
        compiler_params=pltpu.CompilerParams(vmem_limit_bytes=48 * 1024 * 1024),
        name="attend",
    )(starts.reshape(length, 1), received, received, received)


def attend_back_kernel(
    size,
    start_ref,
    query_ref,
    key_ref,
    value_ref,
    grad_ref,
    context_ref,
    logsum_ref,
    out_ref,
    scaled_ref,
    lsum_ref,
    dots_ref,
    gradq_ref,
):
    key_block = pl.program_id(1)
    blocks = pl.num_programs(1)
    length = query_ref.shape[0]

    @pl.when(key_block == 0)
    def _():
        gradq_ref[...] = jnp.zeros_like(gradq_ref)
        scaled_ref[...] = query_ref[...] * jnp.asarray(HD ** (-0.5), jnp.bfloat16)

        def prepare(block, _):
            begin = pl.multiple_of(block * size, size)
            rows = pl.ds(begin, size)
            turned = logsum_ref[rows, :].T
            lsum_ref[0:1, rows] = turned[0:1, :]
            lsum_ref[1:2, rows] = turned[HD : HD + 1, :]
            product = (
                grad_ref[rows, :].astype(jnp.float32) * context_ref[rows, :].astype(jnp.float32)
            ).T
            dots_ref[0:1, rows] = jnp.sum(product[:HD, :], axis=0, keepdims=True)
            dots_ref[1:2, rows] = jnp.sum(product[HD:, :], axis=0, keepdims=True)
            return 0

        lax.fori_loop(0, blocks, prepare, 0)

    key_begin = pl.multiple_of(key_block * size, size)
    key_rows = pl.ds(key_begin, size)
    keys = key_ref[key_rows, :]
    values = value_ref[key_rows, :]
    turned_keys = keys.astype(jnp.float32).T.astype(jnp.bfloat16)
    top = lax.broadcasted_iota(jnp.int32, turned_keys.shape, 0) < HD
    none = jnp.zeros_like(turned_keys)
    turned_both = jnp.concatenate(
        [jnp.where(top, turned_keys, none), jnp.where(top, none, turned_keys)], axis=1
    )
    key_place = lax.broadcasted_iota(jnp.int32, (size, size), 0)

    def step(block, carry, diagonal):
        grad_key, grad_value = carry
        begin = pl.multiple_of(block * size, size)
        rows = pl.ds(begin, size)
        query_heads = head_masks(scaled_ref[rows, :])
        grad_heads = head_masks(grad_ref[rows, :])
        seen = key_place >= start_ref[0:1, rows] - key_begin
        if diagonal:
            seen = seen & (key_place <= lax.broadcasted_iota(jnp.int32, (size, size), 1))
        probs = []
        score_grads = []
        for head in range(2):
            scores = lax.dot_general(
                keys, query_heads[head], NT, preferred_element_type=jnp.float32
            )
            exact = jnp.exp(
                jnp.where(seen, scores - lsum_ref[head : head + 1, rows], HIDDEN)
            )
            prob_grad = lax.dot_general(
                values, grad_heads[head], NT, preferred_element_type=jnp.float32
            )
            probs.append(exact.astype(jnp.bfloat16))
            score_grads.append(
                (exact * (prob_grad - dots_ref[head : head + 1, rows])).astype(jnp.bfloat16)
            )
        grad_value = grad_value + jnp.dot(
            jnp.concatenate(probs, axis=1),
            jnp.concatenate(grad_heads, axis=0),
            preferred_element_type=jnp.float32,
        )
        grad_key = grad_key + jnp.dot(
            jnp.concatenate(score_grads, axis=1),
            jnp.concatenate(query_heads, axis=0),
            preferred_element_type=jnp.float32,
        )
        gradq_ref[:, rows] += jnp.dot(
            turned_both,
            jnp.concatenate(score_grads, axis=0),
            preferred_element_type=jnp.float32,
        )
        return grad_key, grad_value

    empty = jnp.zeros((size, PAIR), jnp.float32)
    carry = step(key_block, (empty, empty), True)
    grad_key, grad_value = lax.fori_loop(
        key_block + 1, blocks, lambda b, c: step(b, c, False), carry
    )
    out_ref[1, key_rows, :] = grad_key.astype(out_ref.dtype)
    out_ref[2, key_rows, :] = grad_value.astype(out_ref.dtype)

    @pl.when(key_block == blocks - 1)
    def _():
        def finish(block, _):
            rows = pl.ds(pl.multiple_of(block * size, size), size)
            out_ref[0, rows, :] = (gradq_ref[:, rows].T * HD ** (-0.5)).astype(out_ref.dtype)
            return 0

        lax.fori_loop(0, blocks, finish, 0)


def attend_back(received, starts, grad_context, context, logsum, pairs):
    length = received.shape[0]
    size = min(BWD_BLOCK, length)
    whole = lambda third: pl.BlockSpec((length, PAIR), lambda p, r, t=third: (0, t * pairs + p))
    pair_work = length * length * PAIR * 4
    return pl.pallas_call(
        partial(attend_back_kernel, size),
        grid=(pairs, length // size),
        in_specs=[
            pl.BlockSpec((1, length), lambda p, r: (0, 0)),
            whole(0),
            whole(1),
            whole(2),
            whole(0),
            whole(0),
            whole(0),
        ],
        out_specs=pl.BlockSpec((3, length, PAIR), lambda p, r: (0, 0, p)),
        out_shape=jax.ShapeDtypeStruct((3, length, pairs * PAIR), jnp.bfloat16),
        scratch_shapes=[
            pltpu.VMEM((length, PAIR), jnp.bfloat16),
            pltpu.VMEM((8, length), jnp.float32),
            pltpu.VMEM((8, length), jnp.float32),
            pltpu.VMEM((PAIR, length), jnp.float32),
        ],
        cost_estimate=pl.CostEstimate(
            flops=pairs * pair_work * 10,
            bytes_accessed=received.size * 8,
            transcendentals=pairs * length * length,
        ),
        compiler_params=pltpu.CompilerParams(vmem_limit_bytes=48 * 1024 * 1024),
        name="attend_back",
    )(starts.reshape(1, length), received, received, received, grad_context, context, logsum)


def local(
    inputs,
    cotangent,
    segments,
    norm1_gain,
    norm1_bias,
    qkv_weight,
    query_bias,
    value_bias,
    proj_weight,
    proj_bias,
    norm2_gain,
    norm2_bias,
    up_weight,
    up_bias,
    down_weight,
    down_bias,
    *,
    devices,
):
    seq_count, own_rows, model_width = inputs.shape
    length = segments.shape[1]
    token_count = seq_count * own_rows
    own_width = model_width // devices
    fold = up_bias.shape[0] // own_width
    groups = devices // seq_count
    pairs = -(-(model_width // PAIR) // groups)
    group_width = pairs * PAIR
    padded = groups * group_width
    place = lax.axis_index("fsdp")
    starts = lax.dynamic_slice_in_dim(segments, place // groups, 1, 0)

    def widen(block):
        spare = [(0, 0)] * (block.ndim - 1) + [(0, padded - model_width)]
        return jnp.pad(block, spare) if padded > model_width else block

    def to_heads(block):
        split = block.reshape(seq_count, own_rows, groups, -1).transpose(0, 2, 1, 3)
        split = split.reshape(devices, own_rows, -1)
        moved = lax.all_to_all(split, "fsdp", split_axis=0, concat_axis=0, tiled=True)
        return moved.reshape(length, -1)

    def by_group(block):
        thirds = widen(block.reshape(-1, 3, model_width))
        return (
            thirds.reshape(-1, 3, groups, group_width).transpose(0, 2, 1, 3).reshape(-1, 3 * padded)
        )

    small = jnp.concatenate(
        [
            jnp.stack(
                [
                    norm1_gain,
                    norm1_bias,
                    query_bias,
                    value_bias,
                    proj_bias,
                    norm2_gain,
                    norm2_bias,
                    down_bias,
                ]
            ),
            up_bias.reshape(fold, own_width),
        ]
    )
    small = jnp.pad(small, ((0, PAIR - small.shape[0]), (0, 0))).T
    first_full = lax.all_gather(
        jnp.concatenate([by_group(qkv_weight), small], axis=1), "fsdp", axis=0, tiled=True
    )
    qkv_full = first_full[:, : 3 * padded]
    vectors = first_full[:, 3 * padded :].T.astype(jnp.float32)
    gain_one, shift_one, query_shift, value_shift = vectors[0], vectors[1], vectors[2], vectors[3]
    proj_shift, gain_two, shift_two, down_shift = vectors[4], vectors[5], vectors[6], vectors[7]
    up_shift = (
        vectors[8 : 8 + fold].reshape(fold, devices, own_width).transpose(1, 0, 2).reshape(-1)
    )
    proj_full = lax.all_gather(proj_weight, "fsdp", axis=0, tiled=True)
    up_full = lax.all_gather(up_weight, "fsdp", axis=0, tiled=True)
    down_full = lax.all_gather(down_weight, "fsdp", axis=0, tiled=True)

    tokens_in = inputs.astype(jnp.float32).reshape(token_count, model_width)
    normed_one = layer_norm_core(tokens_in, gain_one, shift_one).astype(jnp.bfloat16)
    offsets = by_group(
        jnp.concatenate([query_shift, jnp.zeros_like(query_shift), value_shift])[None]
    )
    projected = (
        jnp.dot(normed_one, qkv_full, preferred_element_type=jnp.float32) + offsets
    ).astype(jnp.bfloat16)
    received = to_heads(projected)
    head_context, logsum = attend(received, starts, pairs)

    def to_tokens(block):
        moved = lax.all_to_all(
            block.reshape(devices, own_rows, -1), "fsdp", split_axis=0, concat_axis=0, tiled=True
        )
        moved = moved.reshape(seq_count, groups, own_rows, -1).transpose(0, 2, 1, 3)
        return moved.reshape(token_count, -1)

    mixed = to_tokens(head_context)[:, :model_width]
    attention_out = jnp.dot(mixed, proj_full, preferred_element_type=jnp.float32) + proj_shift
    residual = tokens_in + attention_out
    normed_two = layer_norm_core(residual, gain_two, shift_two).astype(jnp.bfloat16)
    upward = jnp.dot(normed_two, up_full, preferred_element_type=jnp.float32) + up_shift
    activated = smooth_gate(upward).astype(jnp.bfloat16)
    downward = jnp.dot(activated, down_full, preferred_element_type=jnp.float32) + down_shift
    layer_out = (residual + downward).astype(jnp.bfloat16)
    upstream = cotangent.astype(jnp.float32).reshape(token_count, model_width)
    down_grad = cotangent.reshape(token_count, model_width)

    def scatter(grad):
        return lax.psum_scatter(
            grad.astype(jnp.bfloat16), "fsdp", scatter_dimension=0, tiled=True
        )

    own_down = scatter(
        jnp.einsum("nf,nd->fd", activated, down_grad, preferred_element_type=jnp.float32)
    )
    grad_down_shift = jnp.sum(down_grad.astype(jnp.float32), axis=0)
    grad_activated = jnp.einsum(
        "nd,fd->nf", down_grad, down_full, preferred_element_type=jnp.float32
    )
    gate_value, gate_pullback = jax.vjp(smooth_gate, upward)
    up_grad = gate_pullback(grad_activated)[0].astype(jnp.bfloat16)
    own_up = scatter(
        jnp.einsum("nd,nf->df", normed_two, up_grad, preferred_element_type=jnp.float32)
    )
    grad_up_shift = jnp.sum(up_grad.astype(jnp.float32), axis=0)
    grad_normed_two = jnp.einsum("nf,df->nd", up_grad, up_full, preferred_element_type=jnp.float32)
    norm_value, norm_pullback = jax.vjp(layer_norm_core, residual, gain_two, shift_two)
    grad_residual_norm, grad_gain_two, grad_shift_two = norm_pullback(grad_normed_two)
    grad_residual = upstream + grad_residual_norm
    attention_grad = grad_residual.astype(jnp.bfloat16)
    own_proj = scatter(
        jnp.einsum("nd,ne->de", mixed, attention_grad, preferred_element_type=jnp.float32)
    )
    grad_proj_shift = jnp.sum(attention_grad.astype(jnp.float32), axis=0)
    grad_mixed = jnp.einsum(
        "ne,de->nd", attention_grad, proj_full, preferred_element_type=jnp.float32
    ).astype(jnp.bfloat16)
    head_grads = attend_back(
        received, starts, to_heads(widen(grad_mixed)), head_context, logsum, pairs
    )
    moved = lax.all_to_all(
        head_grads.reshape(3, devices, own_rows, group_width),
        "fsdp",
        split_axis=1,
        concat_axis=1,
        tiled=True,
    ).reshape(3, seq_count, groups, own_rows, group_width)
    qkv_grad = moved.transpose(1, 3, 2, 0, 4).reshape(token_count, 3 * padded)
    grad_qkv_weight = jnp.einsum(
        "nd,ne->de", normed_one, qkv_grad, preferred_element_type=jnp.float32
    )
    column_sums = jnp.sum(qkv_grad.astype(jnp.float32), axis=0)
    column_sums = column_sums.reshape(groups, 3, group_width).transpose(1, 0, 2)
    column_sums = column_sums.reshape(3, padded)[:, :model_width]
    grad_normed_one = jnp.einsum(
        "ne,de->nd", qkv_grad, qkv_full, preferred_element_type=jnp.float32
    )
    first_value, first_pullback = jax.vjp(layer_norm_core, tokens_in, gain_one, shift_one)
    grad_input_norm, grad_gain_one, grad_shift_one = first_pullback(grad_normed_one)
    input_grad = grad_residual + grad_input_norm
    early = lax.psum((own_proj, own_up, own_down), "dp")
    small_grads = jnp.concatenate(
        [
            jnp.stack(
                [
                    grad_gain_one,
                    grad_shift_one,
                    column_sums[0],
                    column_sums[2],
                    grad_proj_shift,
                    grad_gain_two,
                    grad_shift_two,
                    grad_down_shift,
                ]
            ),
            grad_up_shift.reshape(devices, fold, own_width)
            .transpose(1, 0, 2)
            .reshape(fold, model_width),
        ]
    )
    small_grads = jnp.pad(small_grads, ((0, PAIR - small_grads.shape[0]), (0, 0))).T
    last = scatter(jnp.concatenate([grad_qkv_weight, small_grads], axis=1))
    last, early = lax.optimization_barrier((last, early))
    last = lax.psum(last, "dp").astype(jnp.float32)
    sum_proj, sum_up, sum_down = (part.astype(jnp.float32) for part in early)
    sum_qkv = last[:, : 3 * padded].reshape(own_width, groups, 3, group_width)
    sum_qkv = sum_qkv.transpose(0, 2, 1, 3).reshape(own_width, 3, padded)[:, :, :model_width]
    sum_qkv = sum_qkv.reshape(own_width, 3 * model_width)
    own = last[:, 3 * padded :].T
    return (
        layer_out.reshape(seq_count, own_rows, model_width),
        input_grad.reshape(seq_count, own_rows, model_width),
        own[0],
        own[1],
        sum_qkv,
        own[2],
        own[3],
        sum_proj,
        own[4],
        own[5],
        own[6],
        sum_up,
        own[8 : 8 + fold].reshape(-1),
        sum_down,
        own[7],
    )


def solution(mesh):
    in_specs = (
        P("dp", "fsdp", None),
        P("dp", "fsdp", None),
        P("dp", None),
        P("fsdp"),
        P("fsdp"),
        P("fsdp", None),
        P("fsdp"),
        P("fsdp"),
        P("fsdp", None),
        P("fsdp"),
        P("fsdp"),
        P("fsdp"),
        P("fsdp", None),
        P("fsdp"),
        P("fsdp", None),
        P("fsdp"),
    )
    out_specs = (
        P("dp", "fsdp", None),
        P("dp", "fsdp", None),
        P("fsdp"),
        P("fsdp"),
        P("fsdp", None),
        P("fsdp"),
        P("fsdp"),
        P("fsdp", None),
        P("fsdp"),
        P("fsdp"),
        P("fsdp"),
        P("fsdp", None),
        P("fsdp"),
        P("fsdp", None),
        P("fsdp"),
    )
    return jax.shard_map(
        partial(local, devices=mesh.shape["fsdp"]),
        mesh=mesh, in_specs=in_specs, out_specs=out_specs, check_vma=False,
    )
```

time: 1660 us -> 669 us (0.40)
  matrix products: 704 us -> 107 us
  waiting for transfers between devices: 572 us -> 328 us
  local copies, waits for them, and re-layouts: 184 us -> 66.6 us
  Pallas kernels: 0 us -> 100 us
  blocking collectives: 73.5 us -> 0 us
  other arithmetic: 85 us -> 24.2 us
  loops' own time: 20.7 us -> 0 us
  starting transfers between devices: 0.44 us -> 18.2 us
    dot_general x48 -> x6, matrix products: 644 us -> 43.8 us  [the longest x1 15.1 us: local(): jnp.einsum('nd,fd->nf', down_grad, down_full, preferred_element_type=jnp....]
    reduce_scatter x5 -> x4, waiting for transfers between devices: 383 us -> 52.7 us  [scatter(): lax.psum_scatter(grad.astype(jnp.bfloat16), 'fsdp', scatter_dimension=0,...]
    all_to_all x0 -> x4, waiting for transfers between devices: none -> 170 us  [the longest x2 81.3 us: to_heads(): lax.all_to_all(split, 'fsdp', split_axis=0, concat_axis=0, tiled=True)]
    pallas_call x0 -> x2, Pallas kernels: none -> 100 us  [the longest x1 57.3 us: attend_back(): pl.pallas_call(partial(attend_back_kernel, size), grid=(pairs, length //...]
    all_gather x5 -> x4, waiting for transfers between devices: 113 us -> 34.1 us  [the longest x1 34.1 us: local(): lax.all_gather(jnp.concatenate([by_group(qkv_weight), small], axis=1), 'f...]
    dynamic_slice x49 -> x1, local copies, waits for them, and re-layouts: 61.8 us -> 0.01 us  [local(): starts = lax.dynamic_slice_in_dim(segments, place // groups, 1, 0)]
    unnamed x2 -> x0, blocking collectives: 51.2 us -> none
    and x12 -> x0, other arithmetic: 34.7 us -> none  [local(): (query_segment[:, :, None] == segments[:, None, :]) & (key_place[None, No...]
  transfers between devices with their start and end apart: 11 -> 14, of which waited for: 8 -> 8; matrix products, arithmetic and copies ran while one was open for 16% -> 23% of each run, Pallas kernels for 0% -> 15%
where the time goes in v1:
time: 669 us; the launch traced here: 660 us
  waiting for transfers between devices  328 us (49%)
  matrix products  107 us (16%)
  Pallas kernels  100 us (15%)
  local copies, waits for them, and re-layouts  66.6 us (10%)
  other arithmetic  24.2 us (4%)
  starting transfers between devices  18.2 us (3%)
  between operations  15.3 us (2%)
    all_to_all x2, waiting for transfers between devices, to_heads(): lax.all_to_all(split, 'fsdp', split_axis=0, concat_axis=0, tiled=True)  81.3 us
    all_to_all x1, waiting for transfers between devices, local(): lax.all_to_all(head_grads.reshape(3, devices, own_rows, group_width), 'fs...  68.4 us
    pallas_call x1, Pallas kernels, attend_back(): pl.pallas_call(partial(attend_back_kernel, size), grid=(pairs, length //...  57.3 us
    reduce_scatter x4, waiting for transfers between devices, scatter(): lax.psum_scatter(grad.astype(jnp.bfloat16), 'fsdp', scatter_dimension=0,...  52.7 us
    pallas_call x1, Pallas kernels, attend(): pl.pallas_call(partial(attend_kernel, size), grid=(pairs, length // size)...  43 us
    psum x1, waiting for transfers between devices, local(): early = lax.psum((own_proj, own_up, own_down), 'dp')  37.6 us
    all_gather x1, waiting for transfers between devices, local(): lax.all_gather(jnp.concatenate([by_group(qkv_weight), small], axis=1), 'f...  34.1 us
    psum x1, waiting for transfers between devices, local(): last = lax.psum(last, 'dp').astype(jnp.float32)  32.1 us
  transfers between devices with their start and end apart: 14, of which 8 were waited for; matrix products, arithmetic and copies ran while one was open for 23% of the time, Pallas kernels for 15%

profile of v1, /device:TPU:0, one launch (start us, length us, event | category | flops | bytes accessed | tf_op | source)
XLA Modules:
  0.0 660.1 jit_solution(1221406597753405888)
XLA Ops:
  9.1 1.1 reshape_reshape.6
  15.2 34.1 %all-gather.5.cloned.1.call-done = bf16[768,2432]{1,0:T(8,128)(2,1)} async-done(((bf16[96,2432]{1,0:T(8,128)(2,1)}), bf16[768,2432]{1,0:T(8,128)(2,1)}) %all-gather.5.cloned.1.call-update) | async-done | bytes 3735568 | tf_op jit(solution)/shard_map/all_gather | solution.py:318
  50.3 1.6 slice_reduce_fusion.2
  52.6 7.5 %add_convert_fusion = bf16[1024,2304]{1,0:T(8,128)(2,1)} fusion(bf16[1024,768]{1,0:T(8,128)(2,1)S(1)} %fusion.15, f32[2304]{0:T(1024)S(1)} %add.142, bf16[768,2432]{1,0:T(8,128)(2,1)} %all-gather.5.cloned.1.call-done), kind=kOutput, calls=%fused_computation.10 | convolution fusion | flops 3628597248 | bytes 9839616 | tf_op jit(solution)/shard_map/dot_general | solution.py:338
  60.1 10.1 %reshape.230 = bf16[4,256,2,1152]{3,2,1,0:T(2,128)(2,1)} reshape(bf16[1024,2304]{1,0:T(8,128)(2,1)} %add_convert_fusion) | data formatting | bytes 9437184 | tf_op jit(solution)/shard_map/reshape | solution.py:289
  70.2 5.3 copy.111
  75.4 4.6 all-to-all-start
  81.0 72.7 %all-to-all-done = bf16[8,256,1152]{2,1,0:T(8,128)(2,1)} async-done(((bf16[8,256,1152]{2,1,0:T(8,128)(2,1)}), bf16[8,256,1152]{2,1,0:T(8,128)(2,1)}, u32[]{:S(2)}, u32[]{:S(2)}) %all-to-all-start) | async-done | bytes 4718624 | tf_op jit(solution)/shard_map/all_to_all | solution.py:291
  153.7 43.0 %attend.1 = (bf16[2048,384]{1,0:T(8,128)(2,1)}, f32[2048,384]{1,0:T(8,128)S(1)}) custom-call(s32[2048,1]{1,0:T(8,128)S(1)} %copy.112.start_ref, bf16[2048,1152]{1,0:T(8,128)(2,1)} %bitcast.16.query_ref.key_ref.value_ref, bf16[2048,1152]{1,0:T(8,128)(2,1)} %bitcast.16.query_ref.key_ref.value_ref, bf16[2048,1152]{1,0:T(8,128)(2,1)} %bitcast.16.query_ref.key_ref.value_ref), custom_call_target="tpu_custom_call" | custom-call | flops 25769803776 | bytes 9437184 | tf_op jit(solution)/shard_map/attend/pallas_call | solution.py:87
  196.7 1.7 copy-done.2
  198.4 4.3 all-to-all-start.1
  203.4 20.3 %all-to-all-done.1 = bf16[8,256,384]{2,1,0:T(8,128)(2,1)} async-done(((bf16[8,256,384]{2,1,0:T(8,128)(2,1)}), bf16[8,256,384]{2,1,0:T(8,128)(2,1)}, u32[]{:S(2)}, u32[]{:S(2)}) %all-to-all-start.1) | async-done | bytes 1572896 | tf_op jit(solution)/shard_map/all_to_all | solution.py:344
  223.7 3.0 copy.113
  227.1 3.4 fusion.36
  230.5 1.6 copy-done.7
  232.7 11.2 %fusion.31 = f32[1024,3072]{1,0:T(8,128)} fusion(bf16[768,3072]{1,0:T(8,128)(2,1)} %all-gather.9.cloned.1.call-done, f32[1024,768]{1,0:T(8,128)} %copy-done.7, f32[768]{0:T(1024)S(1)} %get-tuple-element.36, f32[768]{0:T(1024)S(1)} %get-tuple-element.34, f32[1024]{0:T(1024)S(1)} %fusion.26, f32[1024]{0:T(1024)S(1)} %broadcast_multiply_fusion), kind=kOutput, calls=%fused_computation.88 | convolution fusion | flops 4835770368 | bytes 20461568 | tf_op jit(solution)/shard_map/dot_general | solution.py:354
  243.9 15.1 %fusion.37 = (bf16[3072]{0:T(1024)(128)(2,1)S(1)}, bf16[1024,3072]{1,0:T(8,128)(2,1)S(1)}) fusion(f32[1024,3072]{1,0:T(8,128)} %fusion.31, f32[3072]{0:T(1024)S(1)} %add.153, bf16[1024,768]{1,0:T(8,128)(2,1)S(1)} %bitcast.121, bf16[3072,768]{1,0:T(8,128)(2,1)} %all-gather.11.cloned.1.call-done), kind=kOutput, calls=%fused_computation.93 | convolution fusion | flops 4901041152 | bytes 25184256 | tf_op jit(solution)/shard_map/nd,fd->nf/dot_general | solution.py:370
  259.1 5.7 multiply_reduce_fusion
  264.8 1.5 fusion.35
  268.8 2.5 convolution_convert_fusion.4
  271.4 21.0 %convolution_convert_fusion.1 = bf16[768,3072]{1,0:T(8,128)(2,1)} fusion(bf16[1024,3072]{1,0:T(8,128)(2,1)} %copy-done.32, f32[1024,768]{1,0:T(8,128)} %copy-done.7, f32[768]{0:T(1024)S(1)} %get-tuple-element.36, f32[768]{0:T(1024)S(1)} %get-tuple-element.34, f32[1024]{0:T(1024)S(1)} %fusion.26, f32[1024]{0:T(1024)S(1)} %broadcast_multiply_fusion), kind=kOutput, calls=%fused_computation.12 | convolution fusion | flops 4838129664 | bytes 14170112 | tf_op jit(solution)/shard_map/nd,nf->df/dot_general | solution.py:376
  292.4 3.9 convolution_convert_fusion.3
  296.3 3.4 reshape.240
  299.7 1.4 copy.115
  301.1 3.6 all-to-all-start.2
  304.7 12.3 %convolution_convert_fusion = bf16[3072,768]{1,0:T(8,128)(2,1)} fusion(bf16[1024,768]{1,0:T(8,128)(2,1)S(1)} %bitcast.122, f32[1024,3072]{1,0:T(8,128)} %fusion.31, f32[3072]{0:T(1024)S(1)} %add.153), kind=kOutput, calls=%fused_computation.11 | convolution fusion | flops 4865654784 | bytes 18886656 | tf_op jit(solution)/shard_map/nf,nd->fd/dot_general | solution.py:367
  317.0 8.6 %all-to-all-done.2 = bf16[8,256,384]{2,1,0:T(8,128)(2,1)S(1)} async-done(((bf16[8,256,384]{2,1,0:T(8,128)(2,1)}), bf16[8,256,384]{2,1,0:T(8,128)(2,1)S(1)}, u32[]{:S(2)}, u32[]{:S(2)}) %all-to-all-start.2) | async-done | bytes 1572896 | tf_op jit(solution)/shard_map/all_to_all | solution.py:291
  325.6 57.3 %attend_back.1 = bf16[3,2048,384]{2,1,0:T(8,128)(2,1)} custom-call(s32[1,2048]{1,0:T(1,128)S(1)} %constant_dynamic-slice_fusion.start_ref, bf16[2048,1152]{1,0:T(8,128)(2,1)} %bitcast.16.query_ref.key_ref.value_ref, bf16[2048,1152]{1,0:T(8,128)(2,1)} %bitcast.16.query_ref.key_ref.value_ref, bf16[2048,1152]{1,0:T(8,128)(2,1)} %bitcast.16.query_ref.key_ref.value_ref, ...), custom_call_target="tpu_custom_call" | custom-call | flops 64424509440 | bytes 18874368 | tf_op jit(solution)/shard_map/attend_back/pallas_call | solution.py:222
  382.9 5.2 copy.116
  388.2 4.8 all-to-all-start.3
  393.4 1.8 fusion.20
  395.4 68.4 %all-to-all-done.3 = bf16[3,8,256,384]{3,2,0,1:T(8,128)(2,1)} async-done(((bf16[3,8,256,384]{3,2,0,1:T(8,128)(2,1)}), bf16[3,8,256,384]{3,2,0,1:T(8,128)(2,1)}, u32[]{:S(2)}, u32[]{:S(2)}) %all-to-all-start.3) | async-done | bytes 4718624 | tf_op jit(solution)/shard_map/all_to_all | solution.py:394
  463.8 8.6 %copy.118 = bf16[4,256,2,3,384]{1,0,4,3,2:T(4,128)(2,1)} copy(bf16[4,256,2,3,384]{4,1,3,2,0:T(8,128)(2,1)} %bitcast.31) | data formatting | bytes 9437184 | tf_op jit(solution)/shard_map/transpose | solution.py:401
  472.4 4.0 copy.127
  476.5 4.6 fusion.32
  481.2 1.6 copy-done.9
  482.8 1.7 fusion.16
  484.5 5.2 copy.117
  489.7 3.0 reduce.7
  493.5 6.7 %convolution_convert_fusion.2 = bf16[768,2304]{1,0:T(8,128)(2,1)S(1)} fusion(bf16[1024,768]{1,0:T(8,128)(2,1)} %bitcast.132, bf16[1024,2304]{0,1:T(8,128)(2,1)} %bitcast.127), kind=kOutput, calls=%fused_computation.13 | convolution fusion | flops 3625648128 | bytes 9830400 | tf_op jit(solution)/shard_map/nd,ne->de/dot_general | solution.py:402
  500.2 2.1 pad_maximum_fusion
  502.9 13.5 %add_convert_fusion.1 = bf16[1024,768]{1,0:T(8,128)(2,1)} fusion(f32[1024,768]{1,0:T(8,128)} %copy-done.7, bf16[3072,768]{1,0:T(8,128)(2,1)} %all-gather.11.cloned.1.call-done, f32[768]{0:T(1024)S(1)} %copy-done.30, f32[1024,3072]{1,0:T(8,128)} %fusion.31, f32[3072]{0:T(1024)S(1)} %add.153), kind=kOutput, calls=%fused_computation.40 | convolution fusion | flops 4865654784 | bytes 22035456 | tf_op jit(solution)/shard_map/dot_general | solution.py:356
  516.4 37.6 %all-reduce.8.cloned.1.call-done = (bf16[96,768]{1,0:T(8,128)(2,1)}, bf16[96,3072]{1,0:T(8,128)(2,1)}, bf16[384,768]{1,0:T(8,128)(2,1)}) async-done(((bf16[96,768]{1,0:T(8,128)(2,1)}, bf16[96,3072]{1,0:T(8,128)(2,1)}, bf16[384,768]{1,0:T(8,128)(2,1)}), (bf16[96,768]{1,0:T(8,128)(2,1)}, bf16[96,3072]{1,0:T(8,128)(2,1)}, bf16[384,768]{1,0:T(8,128)(2,1)})) %all-reduce.8.cloned.1.call-update) | async-done | bytes 1327120 | tf_op jit(solution)/shard_map/psum | solution.py:414
  553.9 52.6 %reduce-scatter.5.cloned.1.call-done = bf16[96,2432]{1,0:T(8,128)(2,1)} async-done(((bf16[768,2432]{1,0:T(8,128)(2,1)}), bf16[96,2432]{1,0:T(8,128)(2,1)}) %reduce-scatter.5.cloned.1.call-update) | async-done | bytes 466960 | tf_op jit(solution)/shard_map/reduce_scatter | solution.py:362
  606.6 4.8 add_add_fusion.2
  612.2 1.1 convert_element_type.101
  614.4 32.1 %all-reduce.6.cloned.1.call-done = bf16[96,2432]{1,0:T(8,128)(2,1)} async-done(((bf16[96,2432]{1,0:T(8,128)(2,1)}), bf16[96,2432]{1,0:T(8,128)(2,1)}) %all-reduce.6.cloned.1.call-update) | async-done | bytes 466960 | tf_op jit(solution)/shard_map/psum | solution.py:437
  650.5 1.6 reshape_reshape.7
  (152 shorter events, 22.3 us)
Async XLA Ops:
  7.2 73.4 %copy-start = (s32[4,2048]{1,0:T(4,128)S(1)}, s32[4,2048]{1,0:T(4,128)}, u32[]{:S(2)}) copy-start(s32[4,2048]{1,0:T(4,128)} %param.18) | copy-start | bytes 98308
  7.2 5.9 copy-start.3
  7.2 42.1 %all-gather.5.cloned.1.call-start = ((), (), s32[]{:S(2)}) async-start(), calls=%async_computation.8 | async-start | bytes 4202496 | tf_op jit(solution)/shard_map/all_gather | solution.py:318
  11.7 215.4 %all-gather.7.cloned.1.call-start = ((), (), s32[]{:S(2)}) async-start(), calls=%async_computation.9 | async-start | bytes 1327104 | tf_op jit(solution)/shard_map/all_gather | solution.py:328
  12.4 220.3 %all-gather.9.cloned.1.call-start = ((), (), s32[]{:S(2)}) async-start(), calls=%async_computation.10 | async-start | bytes 5308416 | tf_op jit(solution)/shard_map/all_gather | solution.py:329
  13.4 1.2 copy-start.24
  14.6 0.6 copy-start.26
  14.7 37.9 %copy-start.18 = (f32[1024]{0:T(1024)}, f32[1024]{0:T(1024)S(1)}, u32[]{:S(2)}) copy-start(f32[1024]{0:T(1024)S(1)} %rsqrt.25) | copy-start | bytes 12292
  15.2 37.4 %copy-start.20 = (f32[1,2,4,128]{3,1,2,0:T(2,128)}, f32[1,2,4,128]{3,1,2,0:T(2,128)S(1)}, u32[]{:S(2)}) copy-start(f32[1,2,4,128]{3,1,2,0:T(2,128)S(1)} %copy.124) | copy-start | bytes 12292
  51.9 8.2 %copy-start.16 = (f32[768]{0:T(1024)}, f32[768]{0:T(1024)S(1)}, u32[]{:S(2)}) copy-start(f32[768]{0:T(1024)S(1)} %get-tuple-element.41) | copy-start | bytes 9220
  51.9 8.2 %copy-start.22 = (f32[768]{0:T(1024)}, f32[768]{0:T(1024)S(1)}, u32[]{:S(2)}) copy-start(f32[768]{0:T(1024)S(1)} %get-tuple-element.40) | copy-start | bytes 9220
  75.4 78.3 %all-to-all-start = ((bf16[8,256,1152]{2,1,0:T(8,128)(2,1)}), bf16[8,256,1152]{2,1,0:T(8,128)(2,1)}, u32[]{:S(2)}, u32[]{:S(2)}) async-start(bf16[8,256,1152]{2,1,0:T(8,128)(2,1)} %bitcast.117), calls=%async_computation | async-start | bytes 9437184 | tf_op jit(solution)/shard_map/all_to_all | solution.py:291
  80.0 163.9 %all-gather.11.cloned.1.call-start = ((), (), s32[]{:S(2)}) async-start(), calls=%async_computation.11 | async-start | bytes 5308416 | tf_op jit(solution)/shard_map/all_gather | solution.py:330
  196.7 1.7 copy-start.2
  198.4 25.3 %all-to-all-start.1 = ((bf16[8,256,384]{2,1,0:T(8,128)(2,1)}), bf16[8,256,384]{2,1,0:T(8,128)(2,1)}, u32[]{:S(2)}, u32[]{:S(2)}) async-start(bf16[8,256,384]{2,1,0:T(8,128)(2,1)} %bitcast.17), calls=%async_computation.1 | async-start | bytes 3145728 | tf_op jit(solution)/shard_map/all_to_all | solution.py:344
  202.7 290.4 %reduce-scatter.7.cloned.1.call-start = ((), (), s32[]{:S(2)}) async-start(), calls=%async_computation.13 | async-start | bytes 1327104 | tf_op jit(solution)/shard_map/reduce_scatter | solution.py:362
  227.1 3.4 copy-start.11
  230.5 1.7 copy-start.7
  232.7 11.2 %copy-start.6 = (bf16[4,256,768]{2,1,0:T(8,128)(2,1)S(1)}, bf16[4,256,768]{2,1,0:T(8,128)(2,1)}, u32[]{:S(2)}) copy-start(bf16[4,256,768]{2,1,0:T(8,128)(2,1)} %param.17) | copy-start | bytes 4718596
  243.9 15.2 %copy-start.8 = (f32[1024,768]{1,0:T(8,128)S(1)}, f32[1024,768]{1,0:T(8,128)}, u32[]{:S(2)}) copy-start(f32[1024,768]{1,0:T(8,128)} %copy-done.7) | copy-start | bytes 9437188
  243.9 15.2 %copy-start.31 = (bf16[768,3072]{1,0:T(8,128)(2,1)S(1)}, bf16[768,3072]{1,0:T(8,128)(2,1)}, u32[]{:S(2)}) copy-start(bf16[768,3072]{1,0:T(8,128)(2,1)} %all-gather.9.cloned.1.call-done) | copy-start | bytes 14155780
  259.1 5.7 copy-start.32
  266.3 1.6 copy-start.5
  266.3 2.5 copy-start.12
  271.4 221.7 %reduce-scatter.9.cloned.1.call-start = ((), (), s32[]{:S(2)}) async-start(), calls=%async_computation.14 | async-start | bytes 5308416 | tf_op jit(solution)/shard_map/reduce_scatter | solution.py:362
  301.1 24.5 %all-to-all-start.2 = ((bf16[8,256,384]{2,1,0:T(8,128)(2,1)}), bf16[8,256,384]{2,1,0:T(8,128)(2,1)S(1)}, u32[]{:S(2)}, u32[]{:S(2)}) async-start(bf16[8,256,384]{2,1,0:T(8,128)(2,1)} %bitcast.123), calls=%async_computation.2 | async-start | bytes 3145728 | tf_op jit(solution)/shard_map/all_to_all | solution.py:291
  304.7 188.4 %reduce-scatter.11.cloned.1.call-start = ((), (), s32[]{:S(2)}) async-start(), calls=%async_computation.15 | async-start | bytes 5308416 | tf_op jit(solution)/shard_map/reduce_scatter | solution.py:362
  388.1 5.2 copy-start.4
  388.1 5.2 copy-start.17
  388.1 5.2 copy-start.23
  388.1 5.2 copy-start.25
  388.1 5.3 copy-start.28
  388.2 75.6 %all-to-all-start.3 = ((bf16[3,8,256,384]{3,2,0,1:T(8,128)(2,1)}), bf16[3,8,256,384]{3,2,0,1:T(8,128)(2,1)}, u32[]{:S(2)}, u32[]{:S(2)}) async-start(bf16[3,8,256,384]{3,2,0,1:T(8,128)(2,1)} %copy.116), calls=%async_computation.3 | async-start | bytes 9437184 | tf_op jit(solution)/shard_map/all_to_all | solution.py:394
  393.0 160.9 %all-reduce.8.cloned.1.call-start = ((), (), s32[]{:S(2)}) async-start(), calls=%async_computation.17 | async-start | bytes 2654208 | tf_op jit(solution)/shard_map/psum | solution.py:414
  472.4 4.1 copy-start.21
  472.4 4.1 copy-start.29
  476.4 4.7 copy-start.10
  476.5 4.7 copy-start.27
  476.5 6.3 copy-start.19
  481.1 1.7 copy-start.9
  493.1 113.4 %reduce-scatter.5.cloned.1.call-start = ((), (), s32[]{:S(2)}) async-start(), calls=%async_computation.12 | async-start | bytes 4202496 | tf_op jit(solution)/shard_map/reduce_scatter | solution.py:362
  502.2 0.7 copy-start.30
  502.3 144.2 %all-reduce.6.cloned.1.call-start = ((), (), s32[]{:S(2)}) async-start(), calls=%async_computation.16 | async-start | bytes 933888 | tf_op jit(solution)/shard_map/psum | solution.py:437
  606.6 4.8 copy-start.15
  606.6 5.6 copy-start.14
  606.6 6.7 %copy-start.13 = (bf16[384,768]{1,0:T(8,128)(2,1)S(1)}, bf16[384,768]{1,0:T(8,128)(2,1)}, u32[]{:S(2)}) copy-start(bf16[384,768]{1,0:T(8,128)(2,1)} %get-tuple-element.26) | copy-start | bytes 1769476
  648.5 4.4 copy-start.1
Sparse Core Ops, SparseCore 0:
  11.8 37.4 all-gather.4
  51.2 24.0 all-gather.6
  77.2 65.9 all-gather.8
  144.9 50.1 all-gather.10
  271.5 35.8 reduce-scatter.6
  311.1 53.8 reduce-scatter.8
  368.5 82.8 reduce-scatter.10
  493.2 60.6 all-reduce.7
  557.8 48.6 reduce-scatter.4
  608.8 37.6 all-reduce.5

commit v2 on v1

--- a/solution.py
+++ b/solution.py
@@ -411,7 +411,6 @@
     first_value, first_pullback = jax.vjp(layer_norm_core, tokens_in, gain_one, shift_one)
     grad_input_norm, grad_gain_one, grad_shift_one = first_pullback(grad_normed_one)
     input_grad = grad_residual + grad_input_norm
-    early = lax.psum((own_proj, own_up, own_down), "dp")
     small_grads = jnp.concatenate(
         [
             jnp.stack(
@@ -433,9 +432,9 @@
     )
     small_grads = jnp.pad(small_grads, ((0, PAIR - small_grads.shape[0]), (0, 0))).T
     last = scatter(jnp.concatenate([grad_qkv_weight, small_grads], axis=1))
-    last, early = lax.optimization_barrier((last, early))
-    last = lax.psum(last, "dp").astype(jnp.float32)
-    sum_proj, sum_up, sum_down = (part.astype(jnp.float32) for part in early)
+    last, sum_proj, sum_up, sum_down = (
+        part.astype(jnp.float32) for part in lax.psum((last, own_proj, own_up, own_down), "dp")
+    )
     sum_qkv = last[:, : 3 * padded].reshape(own_width, groups, 3, group_width)
     sum_qkv = sum_qkv.transpose(0, 2, 1, 3).reshape(own_width, 3, padded)[:, :, :model_width]
     sum_qkv = sum_qkv.reshape(own_width, 3 * model_width)

time: 669 us -> 630 us (0.942)
  waiting for transfers between devices: 328 us -> 299 us
  matrix products: 107 us -> 98.5 us
    all_to_all x1, waiting for transfers between devices: 68.4 us -> 47.4 us  [local(): lax.all_to_all(head_grads.reshape(3, devices, own_rows, group_width), 'fs...]
    dot_general x1, matrix products: 21 us -> 10.7 us  [local(): jnp.einsum('nd,nf->df', normed_two, up_grad, preferred_element_type=jnp.f...]
    psum x2 -> x1, waiting for transfers between devices: 69.6 us -> 63.6 us  [local(): lax.psum((last, own_proj, own_up, own_down), 'dp')]
  transfers between devices with their start and end apart: 14 -> 13, of which waited for: 8 -> 7; matrix products, arithmetic and copies ran while one was open for 23% -> 21% of each run, Pallas kernels for 15% -> 16%
where the time goes in v2:
time: 630 us; the launch traced here: 621 us
  waiting for transfers between devices  299 us (47%)
  Pallas kernels  100 us (16%)
  matrix products  98.5 us (16%)
  local copies, waits for them, and re-layouts  67.3 us (11%)
  other arithmetic  23.6 us (4%)
  starting transfers between devices  17.6 us (3%)
  between operations  15.1 us (2%)
    all_to_all x2, waiting for transfers between devices, to_heads(): lax.all_to_all(split, 'fsdp', split_axis=0, concat_axis=0, tiled=True)  82.3 us
    psum x1, waiting for transfers between devices, local(): lax.psum((last, own_proj, own_up, own_down), 'dp')  63.6 us
    pallas_call x1, Pallas kernels, attend_back(): pl.pallas_call(partial(attend_back_kernel, size), grid=(pairs, length //...  57.3 us
    reduce_scatter x4, waiting for transfers between devices, scatter(): lax.psum_scatter(grad.astype(jnp.bfloat16), 'fsdp', scatter_dimension=0,...  48.4 us
    all_to_all x1, waiting for transfers between devices, local(): lax.all_to_all(head_grads.reshape(3, devices, own_rows, group_width), 'fs...  47.4 us
    pallas_call x1, Pallas kernels, attend(): pl.pallas_call(partial(attend_kernel, size), grid=(pairs, length // size)...  43 us
    all_gather x1, waiting for transfers between devices, local(): lax.all_gather(jnp.concatenate([by_group(qkv_weight), small], axis=1), 'f...  34.1 us
    all_to_all x1, waiting for transfers between devices, to_tokens(): lax.all_to_all(block.reshape(devices, own_rows, -1), 'fsdp', split_axis=0...  20.6 us
  transfers between devices with their start and end apart: 13, of which 7 were waited for; matrix products, arithmetic and copies ran while one was open for 21% of the time, Pallas kernels for 16%

profile of v2, /device:TPU:0, one launch (start us, length us, event | category | flops | bytes accessed | tf_op | source)
XLA Modules:
  0.0 621.3 jit_solution(10360543214597378981)
XLA Ops:
  9.1 1.1 reshape_reshape.6
  15.2 34.1 %all-gather.5.cloned.1.call-done = bf16[768,2432]{1,0:T(8,128)(2,1)} async-done(((bf16[96,2432]{1,0:T(8,128)(2,1)}), bf16[768,2432]{1,0:T(8,128)(2,1)}) %all-gather.5.cloned.1.call-update) | async-done | bytes 3735568 | tf_op jit(solution)/shard_map/all_gather | solution.py:318
  50.3 1.6 slice_reduce_fusion.2
  52.6 7.5 %add_convert_fusion = bf16[1024,2304]{1,0:T(8,128)(2,1)} fusion(bf16[1024,768]{1,0:T(8,128)(2,1)S(1)} %fusion.15, f32[2304]{0:T(1024)S(1)} %add.142, bf16[768,2432]{1,0:T(8,128)(2,1)} %all-gather.5.cloned.1.call-done), kind=kOutput, calls=%fused_computation.10 | convolution fusion | flops 3628597248 | bytes 9839616 | tf_op jit(solution)/shard_map/dot_general | solution.py:338
  60.1 10.1 %reshape.230 = bf16[4,256,2,1152]{3,2,1,0:T(2,128)(2,1)} reshape(bf16[1024,2304]{1,0:T(8,128)(2,1)} %add_convert_fusion) | data formatting | bytes 9437184 | tf_op jit(solution)/shard_map/reshape | solution.py:289
  70.2 5.3 copy.111
  75.4 4.6 all-to-all-start
  81.0 72.7 %all-to-all-done = bf16[8,256,1152]{2,1,0:T(8,128)(2,1)} async-done(((bf16[8,256,1152]{2,1,0:T(8,128)(2,1)}), bf16[8,256,1152]{2,1,0:T(8,128)(2,1)}, u32[]{:S(2)}, u32[]{:S(2)}) %all-to-all-start) | async-done | bytes 4718624 | tf_op jit(solution)/shard_map/all_to_all | solution.py:291
  153.7 43.0 %attend.1 = (bf16[2048,384]{1,0:T(8,128)(2,1)}, f32[2048,384]{1,0:T(8,128)S(1)}) custom-call(s32[2048,1]{1,0:T(8,128)S(1)} %copy.112.start_ref, bf16[2048,1152]{1,0:T(8,128)(2,1)} %bitcast.16.query_ref.key_ref.value_ref, bf16[2048,1152]{1,0:T(8,128)(2,1)} %bitcast.16.query_ref.key_ref.value_ref, bf16[2048,1152]{1,0:T(8,128)(2,1)} %bitcast.16.query_ref.key_ref.value_ref), custom_call_target="tpu_custom_call" | custom-call | flops 25769803776 | bytes 9437184 | tf_op jit(solution)/shard_map/attend/pallas_call | solution.py:87
  196.7 1.6 copy-done.2
  198.3 4.5 all-to-all-start.1
  203.2 20.6 %all-to-all-done.1 = bf16[8,256,384]{2,1,0:T(8,128)(2,1)} async-done(((bf16[8,256,384]{2,1,0:T(8,128)(2,1)}), bf16[8,256,384]{2,1,0:T(8,128)(2,1)}, u32[]{:S(2)}, u32[]{:S(2)}) %all-to-all-start.1) | async-done | bytes 1572896 | tf_op jit(solution)/shard_map/all_to_all | solution.py:344
  223.9 3.0 copy.113
  227.2 3.4 fusion.36
  230.7 1.6 copy-done.8
  232.9 11.2 %fusion.31 = f32[1024,3072]{1,0:T(8,128)} fusion(bf16[768,3072]{1,0:T(8,128)(2,1)} %all-gather.9.cloned.1.call-done, f32[1024,768]{1,0:T(8,128)} %copy-done.8, f32[768]{0:T(1024)S(1)} %get-tuple-element.28, f32[768]{0:T(1024)S(1)} %get-tuple-element.26, f32[1024]{0:T(1024)S(1)} %fusion.26, f32[1024]{0:T(1024)S(1)} %broadcast_multiply_fusion), kind=kOutput, calls=%fused_computation.88 | convolution fusion | flops 4835770368 | bytes 20461568 | tf_op jit(solution)/shard_map/dot_general | solution.py:354
  244.1 15.5 %fusion.37 = (bf16[3072]{0:T(1024)(128)(2,1)S(1)}, bf16[1024,3072]{1,0:T(8,128)(2,1)S(1)}) fusion(f32[1024,3072]{1,0:T(8,128)} %fusion.31, f32[3072]{0:T(1024)S(1)} %add.153, bf16[1024,768]{1,0:T(8,128)(2,1)S(1)} %bitcast.121, bf16[3072,768]{1,0:T(8,128)(2,1)} %all-gather.11.cloned.1.call-done), kind=kOutput, calls=%fused_computation.93 | convolution fusion | flops 4901041152 | bytes 25184256 | tf_op jit(solution)/shard_map/nd,fd->nf/dot_general | solution.py:370
  259.7 5.7 multiply_reduce_fusion
  265.4 1.5 fusion.35
  268.5 1.1 copy-done.15
  269.6 2.5 convolution_convert_fusion.4
  272.1 4.3 convolution_convert_fusion.3
  276.4 3.4 reshape.240
  279.8 1.4 copy.115
  281.2 3.6 all-to-all-start.2
  285.5 10.7 %convolution_convert_fusion.1 = bf16[768,3072]{1,0:T(8,128)(2,1)} fusion(bf16[1024,3072]{1,0:T(8,128)(2,1)} %copy-done.34, f32[1024,768]{1,0:T(8,128)} %copy-done.8, f32[768]{0:T(1024)S(1)} %get-tuple-element.28, f32[768]{0:T(1024)S(1)} %get-tuple-element.26, f32[1024]{0:T(1024)S(1)} %fusion.26, f32[1024]{0:T(1024)S(1)} %broadcast_multiply_fusion), kind=kOutput, calls=%fused_computation.12 | convolution fusion | flops 4838129664 | bytes 14170112 | tf_op jit(solution)/shard_map/nd,nf->df/dot_general | solution.py:376
  296.2 9.6 %all-to-all-done.2 = bf16[8,256,384]{2,1,0:T(8,128)(2,1)S(1)} async-done(((bf16[8,256,384]{2,1,0:T(8,128)(2,1)}), bf16[8,256,384]{2,1,0:T(8,128)(2,1)S(1)}, u32[]{:S(2)}, u32[]{:S(2)}) %all-to-all-start.2) | async-done | bytes 1572896 | tf_op jit(solution)/shard_map/all_to_all | solution.py:291
  305.8 57.3 %attend_back.1 = bf16[3,2048,384]{2,1,0:T(8,128)(2,1)} custom-call(s32[1,2048]{1,0:T(1,128)S(1)} %constant_dynamic-slice_fusion.start_ref, bf16[2048,1152]{1,0:T(8,128)(2,1)} %bitcast.16.query_ref.key_ref.value_ref, bf16[2048,1152]{1,0:T(8,128)(2,1)} %bitcast.16.query_ref.key_ref.value_ref, bf16[2048,1152]{1,0:T(8,128)(2,1)} %bitcast.16.query_ref.key_ref.value_ref, ...), custom_call_target="tpu_custom_call" | custom-call | flops 64424509440 | bytes 18874368 | tf_op jit(solution)/shard_map/attend_back/pallas_call | solution.py:222
  363.1 5.3 copy.116
  368.4 4.6 all-to-all-start.3
  373.1 12.6 %convolution_convert_fusion = bf16[3072,768]{1,0:T(8,128)(2,1)} fusion(bf16[1024,768]{1,0:T(8,128)(2,1)S(1)} %bitcast.122, f32[1024,3072]{1,0:T(8,128)} %fusion.31, f32[3072]{0:T(1024)S(1)} %add.153), kind=kOutput, calls=%fused_computation.11 | convolution fusion | flops 4865654784 | bytes 18886656 | tf_op jit(solution)/shard_map/nf,nd->fd/dot_general | solution.py:367
  387.1 1.8 fusion.20
  389.1 47.4 %all-to-all-done.3 = bf16[3,8,256,384]{3,2,0,1:T(8,128)(2,1)} async-done(((bf16[3,8,256,384]{3,2,0,1:T(8,128)(2,1)}), bf16[3,8,256,384]{3,2,0,1:T(8,128)(2,1)}, u32[]{:S(2)}, u32[]{:S(2)}) %all-to-all-start.3) | async-done | bytes 4718624 | tf_op jit(solution)/shard_map/all_to_all | solution.py:394
  436.5 8.6 %copy.118 = bf16[4,256,2,3,384]{1,0,4,3,2:T(4,128)(2,1)} copy(bf16[4,256,2,3,384]{4,1,3,2,0:T(8,128)(2,1)} %bitcast.31) | data formatting | bytes 9437184 | tf_op jit(solution)/shard_map/transpose | solution.py:401
  445.2 4.0 copy.127
  449.3 4.6 fusion.32
  453.9 1.6 copy-done.10
  455.6 2.0 fusion.16
  457.6 5.2 copy.117
  462.8 3.0 reduce.7
  466.1 6.7 %convolution_convert_fusion.2 = bf16[768,2304]{1,0:T(8,128)(2,1)S(1)} fusion(bf16[1024,768]{1,0:T(8,128)(2,1)} %bitcast.132, bf16[1024,2304]{0,1:T(8,128)(2,1)} %bitcast.127), kind=kOutput, calls=%fused_computation.13 | convolution fusion | flops 3625648128 | bytes 9830400 | tf_op jit(solution)/shard_map/nd,ne->de/dot_general | solution.py:402
  472.8 2.2 pad_maximum_fusion
  475.2 48.3 %reduce-scatter.5.cloned.1.call-done = bf16[96,2432]{1,0:T(8,128)(2,1)} async-done(((bf16[768,2432]{1,0:T(8,128)(2,1)}), bf16[96,2432]{1,0:T(8,128)(2,1)}) %reduce-scatter.5.cloned.1.call-update) | async-done | bytes 466960 | tf_op jit(solution)/shard_map/reduce_scatter | solution.py:362
  523.5 13.8 %add_convert_fusion.1 = bf16[1024,768]{1,0:T(8,128)(2,1)} fusion(f32[1024,768]{1,0:T(8,128)} %copy-done.8, bf16[3072,768]{1,0:T(8,128)(2,1)} %all-gather.11.cloned.1.call-done, f32[768]{0:T(1024)S(1)} %copy-done.32, f32[1024,3072]{1,0:T(8,128)} %fusion.31, f32[3072]{0:T(1024)S(1)} %add.153), kind=kOutput, calls=%fused_computation.40 | convolution fusion | flops 4865654784 | bytes 22035456 | tf_op jit(solution)/shard_map/dot_general | solution.py:356
  537.4 2.8 add_add_fusion.2
  540.2 63.6 %all-reduce.5.cloned.1.call-done = (bf16[96,2432]{1,0:T(8,128)(2,1)}, bf16[96,768]{1,0:T(8,128)(2,1)}, bf16[96,3072]{1,0:T(8,128)(2,1)}, bf16[384,768]{1,0:T(8,128)(2,1)}) async-done(((bf16[96,2432]{1,0:T(8,128)(2,1)}, bf16[96,768]{1,0:T(8,128)(2,1)}, bf16[96,3072]{1,0:T(8,128)(2,1)}, bf16[384,768]{1,0:T(8,128)(2,1)}), (bf16[96,2432]{1,0:T(8,128)(2,1)}, bf16[96,768]{1,0:T(8,128)(2,1)}, ...) | async-done | bytes 1794064 | tf_op jit(solution)/shard_map/psum | solution.py:436
  607.9 1.6 reshape_reshape.7
  610.3 2.2 convert_element_type.100
  (153 shorter events, 21.7 us)
Async XLA Ops:
  7.2 73.4 %copy-start = (s32[4,2048]{1,0:T(4,128)S(1)}, s32[4,2048]{1,0:T(4,128)}, u32[]{:S(2)}) copy-start(s32[4,2048]{1,0:T(4,128)} %param.18) | copy-start | bytes 98308
  7.2 5.9 copy-start.3
  7.2 42.1 %all-gather.5.cloned.1.call-start = ((), (), s32[]{:S(2)}) async-start(), calls=%async_computation.8 | async-start | bytes 4202496 | tf_op jit(solution)/shard_map/all_gather | solution.py:318
  11.7 215.6 %all-gather.7.cloned.1.call-start = ((), (), s32[]{:S(2)}) async-start(), calls=%async_computation.9 | async-start | bytes 1327104 | tf_op jit(solution)/shard_map/all_gather | solution.py:328
  12.4 220.5 %all-gather.9.cloned.1.call-start = ((), (), s32[]{:S(2)}) async-start(), calls=%async_computation.10 | async-start | bytes 5308416 | tf_op jit(solution)/shard_map/all_gather | solution.py:329
  13.4 1.2 copy-start.26
  14.6 0.6 copy-start.28
  14.7 37.9 %copy-start.20 = (f32[1024]{0:T(1024)}, f32[1024]{0:T(1024)S(1)}, u32[]{:S(2)}) copy-start(f32[1024]{0:T(1024)S(1)} %rsqrt.25) | copy-start | bytes 12292
  15.2 37.4 %copy-start.22 = (f32[1,2,4,128]{3,1,2,0:T(2,128)}, f32[1,2,4,128]{3,1,2,0:T(2,128)S(1)}, u32[]{:S(2)}) copy-start(f32[1,2,4,128]{3,1,2,0:T(2,128)S(1)} %copy.124) | copy-start | bytes 12292
  51.9 8.2 %copy-start.18 = (f32[768]{0:T(1024)}, f32[768]{0:T(1024)S(1)}, u32[]{:S(2)}) copy-start(f32[768]{0:T(1024)S(1)} %get-tuple-element.33) | copy-start | bytes 9220
  51.9 8.2 %copy-start.24 = (f32[768]{0:T(1024)}, f32[768]{0:T(1024)S(1)}, u32[]{:S(2)}) copy-start(f32[768]{0:T(1024)S(1)} %get-tuple-element.32) | copy-start | bytes 9220
  75.4 78.3 %all-to-all-start = ((bf16[8,256,1152]{2,1,0:T(8,128)(2,1)}), bf16[8,256,1152]{2,1,0:T(8,128)(2,1)}, u32[]{:S(2)}, u32[]{:S(2)}) async-start(bf16[8,256,1152]{2,1,0:T(8,128)(2,1)} %bitcast.117), calls=%async_computation | async-start | bytes 9437184 | tf_op jit(solution)/shard_map/all_to_all | solution.py:291
  80.0 164.0 %all-gather.11.cloned.1.call-start = ((), (), s32[]{:S(2)}) async-start(), calls=%async_computation.11 | async-start | bytes 5308416 | tf_op jit(solution)/shard_map/all_gather | solution.py:330
  196.7 1.6 copy-start.2
  198.3 25.6 %all-to-all-start.1 = ((bf16[8,256,384]{2,1,0:T(8,128)(2,1)}), bf16[8,256,384]{2,1,0:T(8,128)(2,1)}, u32[]{:S(2)}, u32[]{:S(2)}) async-start(bf16[8,256,384]{2,1,0:T(8,128)(2,1)} %bitcast.17), calls=%async_computation.1 | async-start | bytes 3145728 | tf_op jit(solution)/shard_map/all_to_all | solution.py:344
  227.2 3.4 copy-start.13
  230.6 1.7 copy-start.8
  232.9 11.2 %copy-start.7 = (bf16[4,256,768]{2,1,0:T(8,128)(2,1)S(1)}, bf16[4,256,768]{2,1,0:T(8,128)(2,1)}, u32[]{:S(2)}) copy-start(bf16[4,256,768]{2,1,0:T(8,128)(2,1)} %param.17) | copy-start | bytes 4718596
  244.1 15.6 %copy-start.9 = (f32[1024,768]{1,0:T(8,128)S(1)}, f32[1024,768]{1,0:T(8,128)}, u32[]{:S(2)}) copy-start(f32[1024,768]{1,0:T(8,128)} %copy-done.8) | copy-start | bytes 9437188
  244.1 15.6 %copy-start.33 = (bf16[768,3072]{1,0:T(8,128)(2,1)S(1)}, bf16[768,3072]{1,0:T(8,128)(2,1)}, u32[]{:S(2)}) copy-start(bf16[768,3072]{1,0:T(8,128)(2,1)} %all-gather.9.cloned.1.call-done) | copy-start | bytes 14155780
  259.6 5.7 copy-start.34
  266.9 1.6 copy-start.5
  266.9 2.8 copy-start.14
  268.5 1.1 copy-start.15
  281.2 24.5 %all-to-all-start.2 = ((bf16[8,256,384]{2,1,0:T(8,128)(2,1)}), bf16[8,256,384]{2,1,0:T(8,128)(2,1)S(1)}, u32[]{:S(2)}, u32[]{:S(2)}) async-start(bf16[8,256,384]{2,1,0:T(8,128)(2,1)} %bitcast.123), calls=%async_computation.2 | async-start | bytes 3145728 | tf_op jit(solution)/shard_map/all_to_all | solution.py:291
  284.8 190.3 %reduce-scatter.7.cloned.1.call-start = ((), (), s32[]{:S(2)}) async-start(), calls=%async_computation.13 | async-start | bytes 1327104 | tf_op jit(solution)/shard_map/reduce_scatter | solution.py:362
  285.4 189.7 %reduce-scatter.9.cloned.1.call-start = ((), (), s32[]{:S(2)}) async-start(), calls=%async_computation.14 | async-start | bytes 5308416 | tf_op jit(solution)/shard_map/reduce_scatter | solution.py:362
  368.4 68.1 %all-to-all-start.3 = ((bf16[3,8,256,384]{3,2,0,1:T(8,128)(2,1)}), bf16[3,8,256,384]{3,2,0,1:T(8,128)(2,1)}, u32[]{:S(2)}, u32[]{:S(2)}) async-start(bf16[3,8,256,384]{3,2,0,1:T(8,128)(2,1)} %copy.116), calls=%async_computation.3 | async-start | bytes 9437184 | tf_op jit(solution)/shard_map/all_to_all | solution.py:394
  373.0 102.1 %reduce-scatter.11.cloned.1.call-start = ((), (), s32[]{:S(2)}) async-start(), calls=%async_computation.15 | async-start | bytes 5308416 | tf_op jit(solution)/shard_map/reduce_scatter | solution.py:362
  385.7 1.4 copy-start.4
  385.7 1.4 copy-start.19
  385.7 1.4 copy-start.25
  385.7 1.4 copy-start.27
  385.7 1.4 copy-start.30
  385.7 137.7 %reduce-scatter.5.cloned.1.call-start = ((), (), s32[]{:S(2)}) async-start(), calls=%async_computation.12 | async-start | bytes 4202496 | tf_op jit(solution)/shard_map/reduce_scatter | solution.py:362
  445.2 4.1 copy-start.23
  445.2 4.1 copy-start.31
  449.2 4.7 copy-start.12
  449.3 4.7 copy-start.29
  449.3 6.3 %copy-start.21 = (f32[1024]{0:T(1024)S(1)}, f32[1024]{0:T(1024)}, u32[]{:S(2)}) copy-start(f32[1024]{0:T(1024)} %copy-done.20) | copy-start | bytes 12292
  453.9 1.7 copy-start.10
  475.0 48.5 %copy-start.32 = (f32[768]{0:T(1024)S(1)}, f32[768]{0:T(1024)}, u32[]{:S(2)}) copy-start(f32[768]{0:T(1024)} %get-tuple-element.27) | copy-start | bytes 9220
  475.0 128.8 %all-reduce.5.cloned.1.call-start = ((), (), s32[]{:S(2)}) async-start(), calls=%async_computation.16 | async-start | bytes 3588096 | tf_op jit(solution)/shard_map/psum | solution.py:436
  523.5 13.9 %copy-start.6 = (f32[1024,768]{1,0:T(8,128)S(1)}, f32[1024,768]{1,0:T(8,128)}, u32[]{:S(2)}) copy-start(f32[1024,768]{1,0:T(8,128)} %copy-done.5) | copy-start | bytes 9437188
  523.5 13.9 %copy-start.11 = (f32[1024,768]{1,0:T(8,128)S(1)}, f32[1024,768]{1,0:T(8,128)}, u32[]{:S(2)}) copy-start(f32[1024,768]{1,0:T(8,128)} %copy-done.10) | copy-start | bytes 9437188
  606.0 3.5 copy-start.17
  607.4 5.8 copy-start.16
  607.4 6.9 %copy-start.1 = (s32[4,2048]{1,0:T(4,128)S(1)}, s32[4,2048]{1,0:T(4,128)}, u32[]{:S(2)}) copy-start(s32[4,2048]{1,0:T(4,128)} %param.18) | copy-start | bytes 98308
Sparse Core Ops, SparseCore 0:
  11.8 37.4 all-gather.4
  51.2 24.0 all-gather.6
  77.2 65.9 all-gather.8
  144.9 50.1 all-gather.10
  289.1 38.1 reduce-scatter.6
  331.0 60.1 reduce-scatter.8
  394.6 67.6 reduce-scatter.10
  475.1 48.2 reduce-scatter.4
  526.1 77.6 all-reduce.4
